TPU v7x, 256 devices: a whole 4x4x8 slice. The times are simulated.
256 devices in a mesh: brow: 16 (over x, y_hi, core), bcol: 16 (over y_lo, z).
Axes of the slice: x: 4, y: 4 (y_hi: 2, y_lo: 2; y = y_hi * 2 + y_lo), z: 8, core: 2. Of those that a mesh axis runs over, the one named last changes fastest.
Arguments:
- inverse_block: float32 [8192, 8192], P('brow', 'bcol'), may hold values from -8 to 8
- panels: float32 [2, 8192, 2048], P(None, 'bcol', 'brow'), may hold values from -0.06629126 to 0.06629126
- ancestor_blocks: int32 [2, 32], replicated, may hold values 0 or 1
- pattern: int32 [32, 32], P('brow', 'bcol'), may hold values 0 or 1
- diag_inverse: float32 [2, 2048, 2048], P(None, 'brow', 'bcol'), may hold values from -6 to 6
Outputs:
- sigma_ij: float32 [2, 8192, 2048], P(None, 'brow', 'bcol')
- sigma_jj: float32 [2, 2048, 2048], P(None, 'brow', 'bcol')
All inputs are finite; a program needn't handle non-finite values. No bound on the sum of `pattern` on one device may be relied on, other than what follows from the above.
Results may differ from a plain program's by a relative error of at most 0.0001.
Values sent between devices are 32-bit elements; how exact they have to be, the bound alone decides.
A program may use at most 128 MiB of HBM per device.

v0:
```python
import jax
import jax.numpy as jnp
from jax import lax
from jax.sharding import PartitionSpec as P

BLOCK = 256
SNODES = 2


def broadcast(block, axis, source):
    block = jnp.where(lax.axis_index(axis) == source, block, jnp.zeros_like(block))
    return lax.psum(block, axis)


def keep_rows(flags, first_block, count_rows, blk):
    picked = lax.dynamic_slice_in_dim(flags, first_block, count_rows // blk, 0)
    return jnp.repeat(picked.astype(jnp.float32), blk)[:, None]


def on_device(inverse_block, panels, ancestor_blocks, pattern, diag_inverse):
    blk = BLOCK
    rows_here, cols_here = inverse_block.shape
    sparse_inv = (
        inverse_block.reshape(rows_here // blk, blk, cols_here // blk, blk)
        * pattern.astype(jnp.float32)[:, None, :, None]
    ).reshape(rows_here, cols_here)
    row_index = lax.axis_index("brow")
    col_index = lax.axis_index("bcol")
    ratio = lax.axis_size("brow") // lax.axis_size("bcol")
    panel_rows = panels.shape[1]
    root = row_index // ratio
    col_first = col_index * (panel_rows // blk)
    row_first = row_index * (rows_here // blk)
    col_keep = [keep_rows(ancestor_blocks[s], col_first, panel_rows, blk) for s in range(SNODES)]
    row_keep = [keep_rows(ancestor_blocks[s], row_first, rows_here, blk) for s in range(SNODES)]
    locals_masked = [panels[s] * col_keep[s] for s in range(SNODES)]
    outer = []
    inner = []
    for s in range(SNODES):
        gathered = lax.all_gather(locals_masked[s], "brow", axis=1, tiled=True)
        summed = lax.psum_scatter(
            jnp.dot(
                sparse_inv,
                gathered,
                precision=lax.Precision.HIGHEST,
                preferred_element_type=jnp.float32,
            ),
            "bcol",
            scatter_dimension=1,
            tiled=True,
        )
        owned = broadcast(gathered, "bcol", root)
        cross = -summed * row_keep[s]
        diag_term = lax.psum_scatter(
            jnp.dot(
                owned.T, cross, precision=lax.Precision.HIGHEST, preferred_element_type=jnp.float32
            ),
            "brow",
            scatter_dimension=0,
            tiled=True,
        )
        outer.append(cross)
        inner.append(diag_inverse[s] - diag_term)
    return (jnp.stack(outer), jnp.stack(inner))


def solution(mesh):
    return jax.shard_map(
        on_device,
        mesh=mesh,
        in_specs=(
            P("brow", "bcol"),
            P(None, "bcol", "brow"),
            P(),
            P("brow", "bcol"),
            P(None, "brow", "bcol"),
        ),
        out_specs=(P(None, "brow", "bcol"), P(None, "brow", "bcol")),
        check_vma=False,
    )
```

profile of v0, /device:TPU:5, one launch (start us, length us, event | category | flops | bytes accessed | tf_op | source)
XLA Modules:
  0.0 663.7 jit_solution(4453151844280956015)
XLA Ops:
  7.2 0.0 copy-start
  7.2 0.0 all-gather.3.cloned.1.call-start
  7.2 0.8 fusion.20
  8.0 0.1 fusion.15
  8.1 0.1 broadcast_bitcast_fusion.3
  8.2 0.1 broadcast_bitcast_fusion.1
  8.2 2.0 bitcast_multiply_fusion.1
  10.3 0.0 all-gather.3.cloned.1.call-update
  10.3 0.0 all-gather.5.cloned.1.call-start
  10.3 0.7 all-gather.5.cloned.1.call-update
  11.0 0.0 reduce-scatter.5.cloned.1.call-start
  11.1 0.7 convert_element_type.27
  11.8 0.3 mul.57
  12.1 0.1 copy.7
  12.2 64.9 %all-gather.3.cloned.1.call-done = f32[512,2048]{1,0:T(8,128)} async-done(((f32[512,128]{1,0:T(8,128)}), f32[512,2048]{1,0:T(8,128)}) %all-gather.3.cloned.1.call-update) | async-done | bytes 4194320 | tf_op jit(solution)/shard_map/all_gather | solution.py:40
  77.1 0.0 copy-done
  77.1 10.1 %fusion.2 = f32[512,2048]{1,0:T(8,128)} fusion(f32[512,2048]{1,0:T(8,128)} %all-gather.3.cloned.1.call-done, f32[512,512]{1,0:T(8,128)S(1)} %copy-done, f32[512,512]{1,0:T(8,128)S(1)} %bitcast.47), kind=kOutput, calls=%fused_computation.5 | convolution fusion | flops 6442713088 | bytes 10485760 | tf_op jit(solution)/shard_map/dot_general | solution.py:42
  87.2 0.0 reduce-scatter.5.cloned.1.call-update
  87.2 0.0 all-reduce.3.cloned.1.call-start
  87.3 2.5 broadcast_select_fusion.1
  89.7 52.8 %all-gather.5.cloned.1.call-done = f32[512,2048]{1,0:T(8,128)} async-done(((f32[512,128]{1,0:T(8,128)}), f32[512,2048]{1,0:T(8,128)}) %all-gather.5.cloned.1.call-update) | async-done | bytes 4194320 | tf_op jit(solution)/shard_map/all_gather | solution.py:40
  142.5 2.5 broadcast_select_fusion
  145.1 0.0 all-reduce.3.cloned.1.call-update
  145.1 0.0 reduce-scatter.7.cloned.1.call-start
  145.1 10.1 %fusion = f32[512,2048]{1,0:T(8,128)} fusion(f32[512,2048]{1,0:T(8,128)} %all-gather.5.cloned.1.call-done, f32[512,512]{1,0:T(8,128)S(1)} %copy-done, f32[512,512]{1,0:T(8,128)S(1)} %bitcast.48), kind=kOutput, calls=%fused_computation.3 | convolution fusion | flops 6442713088 | bytes 10485760 | tf_op jit(solution)/shard_map/dot_general | solution.py:42
  155.3 0.0 reduce-scatter.7.cloned.1.call-update
  155.3 0.2 reduce-scatter.9.cloned.1.call-start
  155.5 0.1 broadcast_bitcast_fusion.2
  155.6 59.5 %reduce-scatter.5.cloned.1.call-done = f32[512,128]{1,0:T(8,128)} async-done(((f32[512,2048]{1,0:T(8,128)}), f32[512,128]{1,0:T(8,128)}) %reduce-scatter.5.cloned.1.call-update) | async-done | bytes 262160 | tf_op jit(solution)/shard_map/reduce_scatter | solution.py:41
  215.1 210.4 %all-reduce.3.cloned.1.call-done = (f32[512,2048]{1,0:T(8,128)}, f32[512,2048]{1,0:T(8,128)}) async-done(((f32[512,2048]{1,0:T(8,128)}, f32[512,2048]{1,0:T(8,128)}), (f32[512,2048]{1,0:T(8,128)}, f32[512,2048]{1,0:T(8,128)})) %all-reduce.3.cloned.1.call-update) | async-done | bytes 8388624 | tf_op jit(solution)/shard_map/psum | solution.py:12
  425.5 10.0 %fusion.4 = f32[2048,128]{1,0:T(8,128)} fusion(f32[512,2048]{1,0:T(8,128)} %get-tuple-element.3, f32[512,128]{1,0:T(8,128)} %reduce-scatter.5.cloned.1.call-done, f32[512]{0:T(512)S(1)} %bitcast.50), kind=kOutput, calls=%fused_computation.11 | convolution fusion | flops 1610743808 | bytes 5507072 | tf_op jit(solution)/shard_map/dot_general | solution.py:55
  435.5 0.0 copy-start.1
  435.5 0.0 reduce-scatter.9.cloned.1.call-update
  435.5 0.3 reduce-scatter.11.cloned.1.call-start
  435.8 0.1 broadcast_bitcast_fusion
  435.9 59.7 %reduce-scatter.7.cloned.1.call-done = f32[512,128]{1,0:T(8,128)} async-done(((f32[512,2048]{1,0:T(8,128)}), f32[512,128]{1,0:T(8,128)}) %reduce-scatter.7.cloned.1.call-update) | async-done | bytes 262160 | tf_op jit(solution)/shard_map/reduce_scatter | solution.py:41
  495.6 10.1 %fusion.6 = f32[2048,128]{1,0:T(8,128)} fusion(f32[512,2048]{1,0:T(8,128)} %get-tuple-element.2, f32[512,128]{1,0:T(8,128)} %reduce-scatter.7.cloned.1.call-done, f32[512]{0:T(512)S(1)} %bitcast.52), kind=kOutput, calls=%fused_computation.13 | convolution fusion | flops 1610743808 | bytes 5507072 | tf_op jit(solution)/shard_map/dot_general | solution.py:55
  505.6 0.0 reduce-scatter.11.cloned.1.call-update
  505.7 0.0 copy-done.2
  505.7 0.1 fusion.7
  505.8 0.0 copy-done.1
  505.8 0.1 fusion.5
  506.0 0.8 pad_maximum_fusion
  506.8 70.2 %reduce-scatter.9.cloned.1.call-done = f32[128,128]{1,0:T(8,128)} async-done(((f32[2048,128]{1,0:T(8,128)}), f32[128,128]{1,0:T(8,128)}) %reduce-scatter.9.cloned.1.call-update) | async-done | bytes 65552 | tf_op jit(solution)/shard_map/reduce_scatter | solution.py:54
  577.0 78.3 %reduce-scatter.11.cloned.1.call-done = f32[128,128]{1,0:T(8,128)} async-done(((f32[2048,128]{1,0:T(8,128)}), f32[128,128]{1,0:T(8,128)}) %reduce-scatter.11.cloned.1.call-update) | async-done | bytes 65552 | tf_op jit(solution)/shard_map/reduce_scatter | solution.py:54
  655.3 0.0 copy-done.3
  655.3 0.9 fusion.11
  656.2 0.7 pad_maximum_fusion.1
  (6 shorter events, 0.0 us)
Async XLA Ops:
  7.2 69.9 %copy-start = (f32[512,512]{1,0:T(8,128)S(1)}, f32[512,512]{1,0:T(8,128)}, u32[]{:S(2)}) copy-start(f32[512,512]{1,0:T(8,128)} %param.5) | copy-start | bytes 3145732
  7.2 69.9 %all-gather.3.cloned.1.call-start = ((), (), s32[]{:S(2)}) async-start(), calls=%async_computation.4 | async-start | bytes 4456448 | tf_op jit(solution)/shard_map/all_gather | solution.py:40
  10.3 132.3 %all-gather.5.cloned.1.call-start = ((), (), s32[]{:S(2)}) async-start(), calls=%async_computation.6 | async-start | bytes 4456448 | tf_op jit(solution)/shard_map/all_gather | solution.py:40
  11.0 204.1 %reduce-scatter.5.cloned.1.call-start = ((), (), s32[]{:S(2)}) async-start(), calls=%async_computation.5 | async-start | bytes 4456448 | tf_op jit(solution)/shard_map/reduce_scatter | solution.py:41
  87.2 338.3 %all-reduce.3.cloned.1.call-start = ((), (), s32[]{:S(2)}) async-start(), calls=%async_computation.10 | async-start | bytes 16777216 | tf_op jit(solution)/shard_map/psum | solution.py:12
  145.1 350.5 %reduce-scatter.7.cloned.1.call-start = ((), (), s32[]{:S(2)}) async-start(), calls=%async_computation.7 | async-start | bytes 4456448 | tf_op jit(solution)/shard_map/reduce_scatter | solution.py:41
  155.3 421.7 %reduce-scatter.9.cloned.1.call-start = ((), (), s32[]{:S(2)}) async-start(), calls=%async_computation.8 | async-start | bytes 1114112 | tf_op jit(solution)/shard_map/reduce_scatter | solution.py:54
  435.5 70.3 %copy-start.1 = (f32[512,128]{1,0:T(8,128)S(1)}, f32[512,128]{1,0:T(8,128)}, u32[]{:S(2)}) copy-start(f32[512,128]{1,0:T(8,128)} %reduce-scatter.5.cloned.1.call-done) | copy-start | bytes 786436
  435.5 219.7 %reduce-scatter.11.cloned.1.call-start = ((), (), s32[]{:S(2)}) async-start(), calls=%async_computation.9 | async-start | bytes 1114112 | tf_op jit(solution)/shard_map/reduce_scatter | solution.py:54
  495.6 10.1 %copy-start.2 = (f32[512,128]{1,0:T(8,128)S(1)}, f32[512,128]{1,0:T(8,128)}, u32[]{:S(2)}) copy-start(f32[512,128]{1,0:T(8,128)} %reduce-scatter.7.cloned.1.call-done) | copy-start | bytes 786436
  495.6 159.7 %copy-start.3 = (f32[2,128,128]{2,1,0:T(8,128)S(1)}, f32[2,128,128]{2,1,0:T(8,128)}, u32[]{:S(2)}) copy-start(f32[2,128,128]{2,1,0:T(8,128)} %param.9) | copy-start | bytes 393220
Sparse Core Ops, SparseCore 0:
  11.1 65.8 all-gather.2
  79.6 62.8 all-gather.4
  145.1 69.9 reduce-scatter.4
  217.7 207.8 all-reduce.2
  427.9 67.6 reduce-scatter.6
  499.6 77.3 reduce-scatter.8
  581.7 73.5 reduce-scatter.10
where the time goes:
time: 667 us; the launch traced here: 664 us
  waiting for transfers between devices  597 us (90%)
  matrix products  40.3 us (6%)
  between operations  14.2 us (2%)
  other arithmetic  10.4 us (2%)
    psum x1, waiting for transfers between devices, broadcast(): return lax.psum(block, axis)  210 us
    reduce_scatter x2, waiting for transfers between devices, on_device(): lax.psum_scatter(jnp.dot(owned.T, cross, precision=lax.Precision.HIGHEST,...  148 us
    reduce_scatter x2, waiting for transfers between devices, on_device(): lax.psum_scatter(jnp.dot(sparse_inv, gathered, precision=lax.Precision.HI...  119 us
    all_gather x2, waiting for transfers between devices, on_device(): gathered = lax.all_gather(locals_masked[s], 'brow', axis=1, tiled=True)  118 us
    dot_general x2, matrix products, on_device(): jnp.dot(sparse_inv, gathered, precision=lax.Precision.HIGHEST, preferred_...  20.3 us
    dot_general x2, matrix products, on_device(): jnp.dot(owned.T, cross, precision=lax.Precision.HIGHEST, preferred_elemen...  20 us
  transfers between devices with their start and end apart: 7, of which 7 were waited for; matrix products, arithmetic and copies ran while one was open for 7% of the time, Pallas kernels for 0%

commit v1 on v0

v1 whole, which is shorter than its diff:
```python
import functools

import jax
import jax.numpy as jnp
from jax import lax
from jax.experimental import pallas as pl
from jax.experimental.pallas import tpu as pltpu
from jax.sharding import PartitionSpec as P

MESH = pl.DeviceIdType.MESH
F32, BF16 = jnp.float32, jnp.bfloat16
BLOCK = 256
ROWS, COLS, HALF = 512, 128, 256


def split(value):
    high = value.astype(BF16)
    return high, (value - high.astype(F32)).astype(BF16)


def dot(a, b):
    return jnp.dot(a, b, preferred_element_type=F32)


def landed(ref, sem):
    pltpu.make_async_copy(ref, ref, sem).wait()


class Sends:
    def __init__(self):
        self.started = []

    def __call__(self, src, dst, send_sem, recv_sem, device):
        copy = pltpu.make_async_remote_copy(
            src_ref=src, dst_ref=dst, send_sem=send_sem, recv_sem=recv_sem, device_id=device, device_id_type=MESH
        )
        copy.start()
        self.started.append(copy)

    def finish(self):
        for copy in self.started:
            copy.wait_send()


class ReduceScatter:
    def __init__(self, send, part, slots, send_sem, recv_sem, up, down):
        self.send, self.part, self.slots = send, part, slots
        self.send_sem, self.recv_sem = send_sem, recv_sem
        self.to = (up, down)

    def hop(self, way, half, d):
        first = 4 if half == way else 3
        mine = self.part(d if way == 0 else 8 - d, half)
        if d < first:
            slot = self.slots(way, half, d)
            landed(slot, self.recv_sem.at[way, half, d])
            mine[...] = mine[...] + slot[...]
        self.send(
            mine,
            self.slots(way, half, d - 1),
            self.send_sem.at[way, half, d],
            self.recv_sem.at[way, half, d - 1],
            self.to[way],
        )

    def step(self, t):
        for way, half in ((0, 0), (1, 1), (0, 1), (1, 0)):
            first = 4 if half == way else 3
            if first - t >= 1:
                self.hop(way, half, first - t)

    def total(self, half):
        up, down = self.slots(0, half, 0), self.slots(1, half, 0)
        landed(up, self.recv_sem.at[0, half, 0])
        landed(down, self.recv_sem.at[1, half, 0])
        return self.part(0, half)[...] + up[...] + down[...]


def kernel(
    s_ref, p_ref, anc, pat, d_ref, oij, ojj,
    pm, sm, sr, sh, sl, pall, ph, pln, cp, zr, cfin, xr, ct, ot, orr, fin, fr,
    y_s, y_r, s_s, s_r, x_s, x_r, f_s, f_r, c_s, c_r, z_s, z_r, e_s, e_r, t_s, t_r, o_s, o_r, h_s, h_r,
):
    brow, bcol = lax.axis_index("brow"), lax.axis_index("bcol")
    x, yh, c = brow // 4, brow // 2 % 2, brow % 2
    yl, z = bcol // 8, bcol % 8
    y = yh * 2 + yl
    own = x * 2 + c

    def at(x, y, z, c):
        return (x * 4 + (y // 2) * 2 + c, (y % 2) * 8 + z)

    right, left = at((x + 1) % 4, y, z, c), at((x + 3) % 4, y, z, c)
    up, down = at(x, y, (z + 1) % 8, c), at(x, y, (z + 7) % 8, c)
    sibling = at(x, y, z, 1 - c)
    partner = (brow, (1 - yl) * 8 + z)
    low = brow % 8
    diagonal_t = low == z
    diagonal_h = brow == bcol
    send = Sends()

    barrier = pltpu.get_barrier_semaphore()

    def greet(device):
        pl.semaphore_signal(barrier, inc=1, device_id=device, device_id_type=MESH)

    for k in (1, 2, 3):
        greet(at(x, (y + k) % 4, z, c))
    for device in (right, left, up, down, sibling):
        greet(device)
    for k in range(2):
        pl.when(z + 8 * k != brow)(lambda k=k: greet((z + 8 * k, yl * 8 + low)))
        pl.when(jnp.logical_or(brow != bcol, brow // 8 != k))(lambda k=k: greet((bcol, k * 8 + low)))

    for half in range(2):
        rows = pl.ds(half * BLOCK, BLOCK)
        pall[own, y, rows, :] = p_ref[yl, rows, :] * anc[yl, 2 * bcol + half].astype(F32)
        pm[rows, :] = p_ref[1 - yl, rows, :] * anc[1 - yl, 2 * bcol + half].astype(F32)

    pl.semaphore_wait(
        barrier, 12 - jnp.where(diagonal_t, 1, 0) - jnp.where(diagonal_h, 1, 0)
    )

    for k in (1, 3, 2):
        send(pm if k != 2 else pall.at[own, y], pall.at[own, y], y_s.at[k], y_r.at[k], at(x, (y + k) % 4, z, c))

    def spread(r):
        piece = pall.at[own, (y + r) % 4]
        send(piece, piece, x_s.at[0, r], x_r.at[0, r], right)
        send(piece, piece, x_s.at[1, r], x_r.at[1, r], left)

    def share(column, r, k):
        piece = pall.at[column * 2 + c, (y + r) % 4]
        send(piece, piece, c_s.at[k, r], c_r.at[k, r], sibling)

    spread(0)
    share(x, 0, 0)

    for i in range(2):
        for j in range(2):
            block = (pl.ds(i * BLOCK, BLOCK), pl.ds(j * BLOCK, BLOCK))
            sm[block] = s_ref[block] * pat[i, j].astype(F32)

    for r in (1, 3, 2):
        landed(pall.at[own, (y + r) % 4], y_r.at[4 - r])
        spread(r)
        share(x, r, 0)
    for i in range(2):
        rows = pl.ds(i * BLOCK, BLOCK)
        send(sm.at[rows], sr.at[rows], s_s.at[i], s_r.at[i], partner)

    def place(ref, index):
        high, low_part = split(ref[...])
        for k in range(2):
            @pl.when(index == k)
            def _():
                sh[:, pl.ds(k * ROWS, ROWS)] = high
                sl[:, pl.ds(k * ROWS, ROWS)] = low_part

    place(sm, yl)

    before, after, across = (x + 3) % 4, (x + 1) % 4, (x + 2) % 4
    for r in (0, 1, 3, 2):
        from_left, from_right = pall.at[before * 2 + c, (y + r) % 4], pall.at[after * 2 + c, (y + r) % 4]
        landed(from_left, x_r.at[0, r])
        if r in (0, 3):
            send(from_left, from_left, f_s.at[r], f_r.at[r], right)
        share(before, r, 1)
        landed(from_right, x_r.at[1, r])
        if r in (1, 2):
            send(from_right, from_right, f_s.at[r], f_r.at[r], left)
        share(after, r, 2)

    def shared(column, r, k):
        landed(pall.at[column * 2 + 1 - c, (y + r) % 4], c_r.at[k, r])

    for i in range(2):
        rows = pl.ds(i * BLOCK, BLOCK)
        landed(sr.at[rows], s_r.at[i])
    place(sr, 1 - yl)

    def multiply(h):
        def unit(q, carry):
            u = h * 4 + q
            for k in range(4):
                high, low_part = split(pall[u, k])
                block = (u, pl.ds(k % 2 * ROWS, ROWS), pl.ds(k // 2 * COLS, COLS))
                ph[block] = high
                pln[block] = low_part
            for i in range(2):
                rows = pl.ds(i * HALF, HALF)
                a, b, value = sh[rows, :], sl[rows, :], ph[u]
                got = dot(a, pln[u]) + dot(b, value) + dot(a, value)
                for k in range(2):
                    cp[(u // 2) * 4 + k * 2 + u % 2, rows, :] = got[:, k * COLS : (k + 1) * COLS]
            return carry

        lax.fori_loop(0, 4, unit, 0)

    def reduction(h, phase):
        return ReduceScatter(
            send,
            lambda d, half: cp.at[h * 8 + (z + d) % 8, pl.ds(half * HALF, HALF)],
            lambda way, half, d: zr.at[phase, way, half, d],
            z_s.at[phase], z_r.at[phase], up, down,
        )

    def collect(reduced, h):
        for half in range(2):
            rows = pl.ds(half * HALF, HALF)
            keep = anc[yl, 2 * brow + half].astype(F32)
            cfin[h, rows, :] = reduced.total(half) * -keep
        pl.when(jnp.logical_or(jnp.logical_not(diagonal_t), brow // 8 != h))(
            lambda: pltpu.make_async_remote_copy(
                src_ref=cfin.at[h], dst_ref=ct.at[brow // 8], send_sem=t_s.at[h], recv_sem=t_r.at[brow // 8],
                device_id=(z + 8 * h, yl * 8 + low), device_id_type=MESH,
            ).start()
        )

    first = x // 2
    second = 1 - first
    for r in range(4):
        shared(x, r, 0)
        shared(before, r, 1)
        shared(after, r, 2)
    multiply(first)
    one = reduction(first, 0)
    one.step(0)
    one.step(1)
    for r in (0, 1, 3, 2):
        landed(pall.at[across * 2 + c, (y + r) % 4], f_r.at[r])
        share(across, r, 3)
    for r in range(4):
        shared(across, r, 3)
    multiply(second)
    two = reduction(second, 1)
    two.step(0)
    one.step(2)
    two.step(1)
    one.step(3)
    two.step(2)
    collect(one, first)
    two.step(3)
    collect(two, second)

    send(cfin.at[1 - yl], xr, e_s, e_r, partner)
    oij[yl] = cfin[yl]
    mine = brow // 8

    @pl.when(diagonal_t)
    def _():
        ct[mine] = cfin[mine]

    for k in range(2):
        pl.when(z + 8 * k != brow)(lambda k=k: landed(ct.at[k], t_r.at[k]))

    turned = jnp.concatenate([ct[0].T, ct[1].T], axis=1)
    high, low_part = split(turned)
    both = jnp.concatenate([high, low_part], axis=0)

    sh[pl.ds(0, 2 * COLS), :] = both

    def unit(u, carry):
        value = ph[u]
        got = dot(sh[pl.ds(0, 2 * COLS), :], value)
        got = got[:COLS] + got[COLS:] + dot(sh[pl.ds(0, COLS), :], pln[u])
        for k in range(2):
            ot[(u // 2) * 4 + k * 2 + u % 2] = got[:, k * COLS : (k + 1) * COLS]
        return carry

    lax.fori_loop(0, 8, unit, 0)
    three = ReduceScatter(
        send,
        lambda d, half: ot.at[half * 8 + (z + d) % 8],
        lambda way, half, d: orr.at[way, half, d],
        o_s, o_r, up, down,
    )
    for t in range(4):
        three.step(t)

    def home(h):
        return pltpu.make_async_remote_copy(
            src_ref=fin.at[h], dst_ref=fr.at[yl], send_sem=h_s.at[h], recv_sem=h_r.at[yl],
            device_id=(z + 8 * h, brow), device_id_type=MESH,
        )

    def away(h):
        return jnp.logical_or(jnp.logical_not(diagonal_h), yl != h)

    for h in range(2):
        fin[h] = three.total(h)
        pl.when(away(h))(lambda h=h: home(h).start())
    landed(xr, e_r)
    oij[1 - yl] = xr[...]

    @pl.when(diagonal_h)
    def _():
        fr[yl] = fin[yl]

    for k in range(2):
        pl.when(jnp.logical_or(brow != bcol, brow // 8 != k))(lambda k=k: landed(fr.at[k], h_r.at[k]))
        ojj[k] = d_ref[k] - fr[k].T

    for h in range(2):
        pl.when(away(h))(lambda h=h: home(h).wait_send())
        pl.when(jnp.logical_or(jnp.logical_not(diagonal_t), mine != h))(
            lambda h=h: pltpu.make_async_remote_copy(
                src_ref=cfin.at[h], dst_ref=ct.at[mine], send_sem=t_s.at[h], recv_sem=t_r.at[mine],
                device_id=(z + 8 * h, yl * 8 + low), device_id_type=MESH,
            ).wait_send()
        )
    send.finish()


def on_device(inverse_block, panels, ancestor_blocks, pattern, diag_inverse):
    vmem, smem = pl.BlockSpec(memory_space=pltpu.VMEM), pl.BlockSpec(memory_space=pltpu.SMEM)
    dma = pltpu.SemaphoreType.DMA
    semaphores = [(4,), (2,), (2, 4), (4,), (4, 4), (2, 2, 2, 5), (), (2,), (2, 2, 5), (2,)]
    return pl.pallas_call(
        kernel,
        out_shape=(
            jax.ShapeDtypeStruct((2, ROWS, COLS), F32),
            jax.ShapeDtypeStruct((2, COLS, COLS), F32),
        ),
        in_specs=[vmem, vmem, smem, smem, vmem],
        out_specs=(vmem, vmem),
        scratch_shapes=[
            pltpu.VMEM((ROWS, COLS), F32),
            pltpu.VMEM((ROWS, ROWS), F32),
            pltpu.VMEM((ROWS, ROWS), F32),
            pltpu.VMEM((ROWS, 2 * ROWS), BF16),
            pltpu.VMEM((ROWS, 2 * ROWS), BF16),
            pltpu.VMEM((8, 4, ROWS, COLS), F32),
            pltpu.VMEM((8, 2 * ROWS, 2 * COLS), BF16),
            pltpu.VMEM((8, 2 * ROWS, 2 * COLS), BF16),
            pltpu.VMEM((16, ROWS, COLS), F32),
            pltpu.VMEM((2, 2, 2, 4, HALF, COLS), F32),
            pltpu.VMEM((2, ROWS, COLS), F32),
            pltpu.VMEM((ROWS, COLS), F32),
            pltpu.VMEM((2, ROWS, COLS), F32),
            pltpu.VMEM((16, COLS, COLS), F32),
            pltpu.VMEM((2, 2, 4, COLS, COLS), F32),
            pltpu.VMEM((2, COLS, COLS), F32),
            pltpu.VMEM((2, COLS, COLS), F32),
        ]
        + [dma(shape) for shape in semaphores for _ in range(2)],
        compiler_params=pltpu.CompilerParams(
            collective_id=0, has_side_effects=True, vmem_limit_bytes=56 * 2**20
        ),
        cost_estimate=pl.CostEstimate(flops=8 * 10**9, bytes_accessed=3 * 2**20, transcendentals=0),
        name="selected_inverse",
    )(inverse_block, panels, ancestor_blocks, pattern, diag_inverse)


def solution(mesh):
    return jax.shard_map(
        on_device,
        mesh=mesh,
        in_specs=(
            P("brow", "bcol"),
            P(None, "bcol", "brow"),
            P(),
            P("brow", "bcol"),
            P(None, "brow", "bcol"),
        ),
        out_specs=(P(None, "brow", "bcol"), P(None, "brow", "bcol")),
        check_vma=False,
    )
```

time: 667 us -> 168 us (0.25)
  waiting for transfers between devices: 597 us -> 0 us
  Pallas kernels: 0 us -> 163 us
  matrix products: 40.3 us -> 0 us
  between operations: 14.2 us -> 0.65 us
  other arithmetic: 10.4 us -> 0 us
    reduce_scatter x4 -> x0, waiting for transfers between devices: 268 us -> none  [the longest x2 148 us: on_device(): lax.psum_scatter(jnp.dot(owned.T, cross, precision=lax.Precision.HIGHEST,...]
    psum x1 -> x0, waiting for transfers between devices: 210 us -> none  [broadcast(): return lax.psum(block, axis)]
    pallas_call x0 -> x1, Pallas kernels: none -> 163 us  [on_device(): pl.pallas_call(kernel, out_shape=(jax.ShapeDtypeStruct((2, ROWS, COLS), F...]
    all_gather x2 -> x0, waiting for transfers between devices: 118 us -> none  [on_device(): gathered = lax.all_gather(locals_masked[s], 'brow', axis=1, tiled=True)]
    dot_general x4 -> x0, matrix products: 40.3 us -> none  [the longest x2 20.3 us: on_device(): jnp.dot(sparse_inv, gathered, precision=lax.Precision.HIGHEST, preferred_...]
  transfers between devices with their start and end apart: 7 -> 0, of which waited for: 7 -> 0; matrix products, arithmetic and copies ran while one was open for 7% -> 0% of each run, Pallas kernels for 0% -> 0%
where the time goes in v1:
time: 168 us; the launch traced here: 166 us
  Pallas kernels  163 us (97%)
  local copies, waits for them, and re-layouts  2.56 us (2%)
    pallas_call x1, Pallas kernels, on_device(): pl.pallas_call(kernel, out_shape=(jax.ShapeDtypeStruct((2, ROWS, COLS), F...  163 us

profile of v1, /device:TPU:5, one launch (start us, length us, event | category | flops | bytes accessed | tf_op | source)
XLA Modules:
  0.0 165.9 jit_solution(5254219282786245112)
XLA Ops:
  0.6 162.7 %selected_inverse.1 = (f32[2,512,128]{2,1,0:T(8,128)}, f32[2,128,128]{2,1,0:T(8,128)}) custom-call(f32[512,512]{1,0:T(8,128)} %s_ref.1, f32[2,512,128]{2,1,0:T(8,128)} %p_ref.1, s32[2,32]{1,0:T(2,128)} %anc.1, s32[2,2]{1,0:T(2,128)} %pat.1, f32[2,128,128]{2,1,0:T(8,128)} %d_ref.1), custom_call_target="tpu_custom_call" | custom-call | flops 8000000000 | bytes 3145728 | tf_op jit(solution)/shard_map/selected_inverse/pallas_call | solution.py:319
  163.3 0.0 copy-start
  163.3 1.9 %copy.9 = f32[2,512,128]{2,1,0:T(8,128)} copy(f32[2,512,128]{2,1,0:T(8,128)} %get-tuple-element.4) | data formatting | bytes 1048576
  165.2 0.0 copy-done
  165.2 0.7 copy.10
Async XLA Ops:
  163.3 1.9 %copy-start = (f32[2,128,128]{2,1,0:T(8,128)S(1)}, f32[2,128,128]{2,1,0:T(8,128)}, u32[]{:S(2)}) copy-start(f32[2,128,128]{2,1,0:T(8,128)} %get-tuple-element.5) | copy-start | bytes 393220

commit v2 on v1

v2 whole, which is shorter than its diff:
```python
import functools

import jax
import jax.numpy as jnp
from jax import lax
from jax.experimental import pallas as pl
from jax.experimental.pallas import tpu as pltpu
from jax.sharding import PartitionSpec as P

MESH = pl.DeviceIdType.MESH
F32, BF16 = jnp.float32, jnp.bfloat16
BLOCK = 256
ROWS, COLS = 512, 128


def split(value):
    high = value.astype(BF16)
    return high, (value - high.astype(F32)).astype(BF16)


def dot(a, b):
    return jnp.dot(a, b, preferred_element_type=F32)


def landed(ref, sem):
    pltpu.make_async_copy(ref, ref, sem).wait()


class Sends:
    def __init__(self):
        self.started = []

    def __call__(self, src, dst, send_sem, recv_sem, device):
        copy = pltpu.make_async_remote_copy(
            src_ref=src, dst_ref=dst, send_sem=send_sem, recv_sem=recv_sem, device_id=device, device_id_type=MESH
        )
        copy.start()
        self.started.append(copy)

    def finish(self):
        for copy in self.started:
            copy.wait_send()


class ReduceScatter:
    def __init__(self, send, part, slots, send_sem, recv_sem, up, down):
        self.send, self.part, self.slots = send, part, slots
        self.send_sem, self.recv_sem = send_sem, recv_sem
        self.to = (up, down)

    def hop(self, way, half, d):
        first = 4 if half == way else 3
        mine = self.part(d if way == 0 else 8 - d, half)
        if d < first:
            slot = self.slots(way, half, d)
            landed(slot, self.recv_sem.at[way, half, d])
            mine[...] = mine[...] + slot[...]
        self.send(
            mine,
            self.slots(way, half, d - 1),
            self.send_sem.at[way, half, d],
            self.recv_sem.at[way, half, d - 1],
            self.to[way],
        )

    def step(self, t):
        for way, half in ((0, 0), (1, 1), (0, 1), (1, 0)):
            first = 4 if half == way else 3
            if first - t >= 1:
                self.hop(way, half, first - t)

    def total(self, half):
        up, down = self.slots(0, half, 0), self.slots(1, half, 0)
        landed(up, self.recv_sem.at[0, half, 0])
        landed(down, self.recv_sem.at[1, half, 0])
        return self.part(0, half)[...] + up[...] + down[...]


GROUPS = 2
PIECE = ROWS // 8
PART = PIECE // GROUPS
TALL = ROWS // GROUPS
UNITS = [(0, 0), (0, 3), (0, 1), (1, 0), (0, 2), (1, 3), (1, 1), (1, 2)]
PLANE = [(a, b, c) for a in (0, 3, 1, 2) for b in range(2) for c in range(2)]
LINE = [(a, b) for b in range(8) for a in range(2)][1:]


class Ring:
    def __init__(self, send, terms, slots, send_sem, recv_sem, z, to):
        self.send, self.terms, self.slots = send, terms, slots
        self.send_sem, self.recv_sem, self.z, self.to = send_sem, recv_sem, z, to

    def step(self, t):
        d = 4 - t
        for way in range(2):
            mine = self.terms.at[(self.z + (d if way == 0 else 8 - d)) % 8]
            half = pl.ds(way * (PART // 2), PART // 2)
            target = self.slots.at[way, d - 1]
            if d == 4:
                mine, target = mine.at[half], target.at[half]
            else:
                slot, into = self.slots.at[way, d], mine
                if d == 3:
                    slot, into = slot.at[half], mine.at[half]
                landed(slot, self.recv_sem.at[way, d])
                into[...] = into[...] + slot[...]
            self.send(mine, target, self.send_sem.at[way, d], self.recv_sem.at[way, d - 1], self.to[way])

    def total(self):
        for way in range(2):
            landed(self.slots.at[way, 0], self.recv_sem.at[way, 0])
        return self.terms[self.z] + self.slots[0, 0] + self.slots[1, 0]


def kernel(
    s_ref, p_ref, anc, pat, d_ref, oij, ojj,
    pm, sm, sr, sh, sl, pall, ph, pln, cp, zr, cf, cb, xo, ct, lhs, ot, orr, fin, fr,
    y_s, y_r, s_s, s_r, x_s, x_r, f_s, f_r, c_s, c_r, z_s, z_r, b_s, b_r, t_s, t_r, e_s, e_r, o_s, o_r, h_s, h_r,
):
    brow, bcol = lax.axis_index("brow"), lax.axis_index("bcol")
    x, yh, c = brow // 4, brow // 2 % 2, brow % 2
    yl, z = bcol // 8, bcol % 8
    y = yh * 2 + yl
    own = x * 2 + c
    low = brow % 8
    diagonal = brow == bcol

    def at(x, y, z, c):
        return (x * 4 + (y // 2) * 2 + c, (y % 2) * 8 + z)

    def row(a, b, c_steps):
        return (x + a) % 4 * 4 + (yh + b) % 2 * 2 + (c + c_steps) % 2

    def column(a, b):
        return (yl + a) % 2 * 8 + (z + b) % 8

    right, left = at((x + 1) % 4, y, z, c), at((x + 3) % 4, y, z, c)
    up, down = at(x, y, (z + 1) % 8, c), at(x, y, (z + 7) % 8, c)
    sibling = at(x, y, z, 1 - c)
    partner = (brow, (1 - yl) * 8 + z)
    send = Sends()

    barrier = pltpu.get_barrier_semaphore()

    def greet(device):
        pl.semaphore_signal(barrier, inc=1, device_id=device, device_id_type=MESH)

    for steps in PLANE[1:]:
        greet((row(*steps), bcol))
    for steps in LINE:
        greet((brow, column(*steps)))
    greet(at(x, (y + 3 + 2 * yl) % 4, z, c))
    for k in range(2):
        pl.when(jnp.logical_or(brow != bcol, brow // 8 != k))(lambda k=k: greet((bcol, k * 8 + low)))

    for half in range(2):
        rows = pl.ds(half * BLOCK, BLOCK)
        pall[own, y, rows, :] = p_ref[yl, rows, :] * anc[yl, 2 * bcol + half].astype(F32)
        pm[rows, :] = p_ref[1 - yl, rows, :] * anc[1 - yl, 2 * bcol + half].astype(F32)

    pl.semaphore_wait(barrier, 33 - jnp.where(diagonal, 1, 0))

    for k in (1, 3, 2):
        send(pm if k != 2 else pall.at[own, y], pall.at[own, y], y_s.at[k], y_r.at[k], at(x, (y + k) % 4, z, c))

    def spread(r):
        piece = pall.at[own, (y + r) % 4]
        send(piece, piece, x_s.at[0, r], x_r.at[0, r], right)
        send(piece, piece, x_s.at[1, r], x_r.at[1, r], left)

    def share(steps, r):
        piece = pall.at[(x + steps) % 4 * 2 + c, (y + r) % 4]
        send(piece, piece, c_s.at[steps, r], c_r.at[steps, r], sibling)

    spread(0)
    share(0, 0)

    for g in range(GROUPS):
        for p in range(8):
            for k in range(2):
                columns = pl.ds(k * BLOCK, BLOCK)
                sm[g, pl.ds(p * PART, PART), columns] = (
                    s_ref[pl.ds(p * PIECE + g * PART, PART), columns] * pat[p // 4, k].astype(F32)
                )

    def swap(g):
        send(sm.at[g], sr.at[g], s_s.at[g], s_r.at[g], partner)

    def place(g, value, index):
        high, low_part = split(value)
        for k in range(2):
            @pl.when(index == k)
            def _():
                sh[g, :, pl.ds(k * ROWS, ROWS)] = high
                sl[g, :, pl.ds(k * ROWS, ROWS)] = low_part

    for r in (1, 3, 2):
        landed(pall.at[own, (y + r) % 4], y_r.at[4 - r])
        spread(r)
        share(0, r)
    for g in range(GROUPS):
        swap(g)
    for g in range(GROUPS):
        place(g, sm[g], yl)

    def neighbours(r):
        from_left, from_right = pall.at[(x + 3) % 4 * 2 + c, (y + r) % 4], pall.at[(x + 1) % 4 * 2 + c, (y + r) % 4]
        landed(from_left, x_r.at[0, r])
        if r in (0, 3):
            send(from_left, from_left, f_s.at[r], f_r.at[r], right)
        share(3, r)
        landed(from_right, x_r.at[1, r])
        if r in (1, 2):
            send(from_right, from_right, f_s.at[r], f_r.at[r], left)
        share(1, r)

    def opposite(r):
        landed(pall.at[(x + 2) % 4 * 2 + c, (y + r) % 4], f_r.at[r])
        share(2, r)

    def swapped(g):
        landed(sr.at[g], s_r.at[g])
        place(g, sr[g], 1 - yl)

    def prepare(steps):
        for r in range(4):
            landed(pall.at[(x + steps) % 4 * 2 + 1 - c, (y + r) % 4], c_r.at[steps, r])

        def one(q, carry):
            u = (x + steps) % 4 * 2 + q
            for k in range(4):
                high, low_part = split(pall[u, k])
                block = (u, pl.ds(k % 2 * ROWS, ROWS), pl.ds(k // 2 * COLS, COLS))
                ph[block] = high
                pln[block] = low_part
            return carry

        lax.fori_loop(0, 2, one, 0)

    def multiply(n):
        g, steps = UNITS[n]
        for q in range(2):
            u = (x + steps) % 4 * 2 + q
            a, b, value = sh[g], sl[g], ph[u]
            got = dot(a, pln[u]) + dot(b, value) + dot(a, value)
            cp[n, :, :, pl.ds(q * 2 * COLS, 2 * COLS)] = got.reshape(8, PART, 2 * COLS)

    rings = [
        Ring(send, cp.at[n], zr.at[n], z_s.at[n], z_r.at[n], z, (up, down)) for n in range(len(UNITS))
    ]
    keep = -anc[yl, 2 * brow + z // 4].astype(F32)

    def finish(n):
        g, steps = UNITS[n]
        total = rings[n].total() * keep
        for q in range(2):
            for k in range(2):
                j = (x + steps) % 4 * 4 + k * 2 + q
                block = q * 2 + k
                cf[j, pl.ds(g * PART, PART), :] = total[:, block * COLS : (block + 1) * COLS]
        if g == GROUPS - 1:
            for index, (a, b, d) in enumerate(PLANE):
                if a == steps and index:
                    j = row(a, b, d)
                    send(cf.at[j], cb.at[brow], b_s.at[index], b_r.at[index], (j, bcol))

    def onward(index, i):
        return pltpu.make_async_remote_copy(
            src_ref=cb.at[i], dst_ref=ct.at[i // 8, z], send_sem=t_s.at[index // 8, index % 8], recv_sem=t_r.at[i // 8, z],
            device_id=(brow, yl * 8 + i % 8), device_id_type=MESH,
        )

    def relay(steps):
        for index, (a, b, d) in enumerate(PLANE):
            if a != steps:
                continue
            i = (x + 4 - a) % 4 * 4 + (yh + b) % 2 * 2 + (c + d) % 2
            if index:
                landed(cb.at[i], b_r.at[index])
            else:
                cb[i] = cf[i]

            @pl.when(i % 8 == z)
            def _():
                ct[i // 8, z] = cb[i]

            pl.when(i % 8 != z)(lambda: onward(index, i).start())

    neighbours(0)
    neighbours(1)
    for time in range(len(UNITS) + 4):
        if time == 0:
            swapped(0)
            prepare(0)
        if time == 1:
            neighbours(3)
            neighbours(2)
            prepare(3)
        if time == 2:
            prepare(1)
        if time == 3:
            swapped(1)
        if time == 4:
            for r in (0, 1, 3, 2):
                opposite(r)
            prepare(2)
        if time < len(UNITS):
            multiply(time)
            rings[time].step(0)
        for t in (3, 2, 1):
            if 0 <= time - t < len(UNITS):
                rings[time - t].step(t)
        if time >= 4:
            finish(time - 4)
        if time == 9:
            relay(0)
        if time == 10:
            relay(3)
    relay(1)
    relay(2)

    for k in range(2):
        for d in range(1, 8):
            landed(ct.at[k, (z + d) % 8], t_r.at[k, (z + d) % 8])
    for index, (a, b) in enumerate(LINE):
        send(cf.at[column(a, b)], xo.at[yl, z], e_s.at[index], e_r.at[index], (brow, column(a, b)))
    xo[yl, z] = cf[bcol]

    turned = jnp.concatenate([ct[k].reshape(ROWS, COLS).T for k in range(2)], axis=1)
    high, low_part = split(turned)
    lhs[pl.ds(0, COLS), :] = high
    lhs[pl.ds(COLS, COLS), :] = low_part

    def unit(u, carry):
        got = dot(lhs[...], ph[u])
        got = got[:COLS] + got[COLS:] + dot(lhs[pl.ds(0, COLS), :], pln[u])
        for k in range(2):
            ot[(u // 2) * 4 + k * 2 + u % 2] = got[:, k * COLS : (k + 1) * COLS]
        return carry

    lax.fori_loop(0, 8, unit, 0)
    last = ReduceScatter(
        send,
        lambda d, half: ot.at[half * 8 + (z + d) % 8],
        lambda way, half, d: orr.at[way, half, d],
        o_s, o_r, up, down,
    )
    for t in range(4):
        last.step(t)

    def home(h):
        return pltpu.make_async_remote_copy(
            src_ref=fin.at[h], dst_ref=fr.at[yl], send_sem=h_s.at[h], recv_sem=h_r.at[yl],
            device_id=(z + 8 * h, brow), device_id_type=MESH,
        )

    def away(h):
        return jnp.logical_or(jnp.logical_not(diagonal), yl != h)

    for h in range(2):
        fin[h] = last.total(h)
        pl.when(away(h))(lambda h=h: home(h).start())
    for index, (a, b) in enumerate(LINE):
        landed(xo.at[(yl + a) % 2, (z + 8 - b) % 8], e_r.at[index])
    oij[...] = xo[...].reshape(2, ROWS, COLS)

    @pl.when(diagonal)
    def _():
        fr[yl] = fin[yl]

    for k in range(2):
        pl.when(jnp.logical_or(brow != bcol, brow // 8 != k))(lambda k=k: landed(fr.at[k], h_r.at[k]))
        ojj[k] = d_ref[k] - fr[k].T

    for h in range(2):
        pl.when(away(h))(lambda h=h: home(h).wait_send())
    for index, (a, b, d) in enumerate(PLANE):
        i = (x + 4 - a) % 4 * 4 + (yh + b) % 2 * 2 + (c + d) % 2
        pl.when(i % 8 != z)(lambda: onward(index, i).wait_send())
    send.finish()


def on_device(inverse_block, panels, ancestor_blocks, pattern, diag_inverse):
    vmem, smem = pl.BlockSpec(memory_space=pltpu.VMEM), pl.BlockSpec(memory_space=pltpu.SMEM)
    dma = pltpu.SemaphoreType.DMA
    count = len(UNITS)
    semaphores = [
        (4,), (GROUPS,), (2, 4), (4,), (4, 4), (count, 2, 5), (16,), (2, 8), (15,), (2, 2, 5), (2,)
    ]
    return pl.pallas_call(
        kernel,
        out_shape=(
            jax.ShapeDtypeStruct((2, ROWS, COLS), F32),
            jax.ShapeDtypeStruct((2, COLS, COLS), F32),
        ),
        in_specs=[vmem, vmem, smem, smem, vmem],
        out_specs=(vmem, vmem),
        scratch_shapes=[
            pltpu.VMEM((ROWS, COLS), F32),
            pltpu.VMEM((GROUPS, TALL, ROWS), F32),
            pltpu.VMEM((GROUPS, TALL, ROWS), F32),
            pltpu.VMEM((GROUPS, TALL, 2 * ROWS), BF16),
            pltpu.VMEM((GROUPS, TALL, 2 * ROWS), BF16),
            pltpu.VMEM((8, 4, ROWS, COLS), F32),
            pltpu.VMEM((8, 2 * ROWS, 2 * COLS), BF16),
            pltpu.VMEM((8, 2 * ROWS, 2 * COLS), BF16),
            pltpu.VMEM((count, 8, PART, 4 * COLS), F32),
            pltpu.VMEM((count, 2, 4, PART, 4 * COLS), F32),
            pltpu.VMEM((16, PIECE, COLS), F32),
            pltpu.VMEM((16, PIECE, COLS), F32),
            pltpu.VMEM((2, 8, PIECE, COLS), F32),
            pltpu.VMEM((2, 8, PIECE, COLS), F32),
            pltpu.VMEM((2 * COLS, 2 * ROWS), BF16),
            pltpu.VMEM((16, COLS, COLS), F32),
            pltpu.VMEM((2, 2, 4, COLS, COLS), F32),
            pltpu.VMEM((2, COLS, COLS), F32),
            pltpu.VMEM((2, COLS, COLS), F32),
        ]
        + [dma(shape) for shape in semaphores for _ in range(2)],
        compiler_params=pltpu.CompilerParams(
            collective_id=0, has_side_effects=True, vmem_limit_bytes=56 * 2**20
        ),
        cost_estimate=pl.CostEstimate(flops=8 * 10**9, bytes_accessed=3 * 2**20, transcendentals=0),
        name="selected_inverse",
    )(inverse_block, panels, ancestor_blocks, pattern, diag_inverse)


def solution(mesh):
    return jax.shard_map(
        on_device,
        mesh=mesh,
        in_specs=(
            P("brow", "bcol"),
            P(None, "bcol", "brow"),
            P(),
            P("brow", "bcol"),
            P(None, "brow", "bcol"),
        ),
        out_specs=(P(None, "brow", "bcol"), P(None, "brow", "bcol")),
        check_vma=False,
    )
```

time: 168 us -> 156 us (0.929); the launches traced: 166 us -> 156 us
  Pallas kernels: 163 us -> 153 us
    pallas_call x1, Pallas kernels: 163 us -> 153 us  [on_device(): pl.pallas_call(kernel, out_shape=(jax.ShapeDtypeStruct((2, ROWS, COLS), F...]
where the time goes in v2:
time: 156 us
  Pallas kernels  153 us (98%)
  local copies, waits for them, and re-layouts  2.56 us (2%)
    pallas_call x1, Pallas kernels, on_device(): pl.pallas_call(kernel, out_shape=(jax.ShapeDtypeStruct((2, ROWS, COLS), F...  153 us

profile of v2, /device:TPU:5, one launch (start us, length us, event | category | flops | bytes accessed | tf_op | source)
XLA Modules:
  0.0 156.3 jit_solution(7871161315412222577)
XLA Ops:
  0.6 153.1 %selected_inverse.1 = (f32[2,512,128]{2,1,0:T(8,128)}, f32[2,128,128]{2,1,0:T(8,128)}) custom-call(f32[512,512]{1,0:T(8,128)} %s_ref.1, f32[2,512,128]{2,1,0:T(8,128)} %p_ref.1, s32[2,32]{1,0:T(2,128)} %anc.1, s32[2,2]{1,0:T(2,128)} %pat.1, f32[2,128,128]{2,1,0:T(8,128)} %d_ref.1), custom_call_target="tpu_custom_call" | custom-call | flops 8000000000 | bytes 3145728 | tf_op jit(solution)/shard_map/selected_inverse/pallas_call | solution.py:390
  153.7 0.0 copy-start
  153.8 1.9 %copy.9 = f32[2,512,128]{2,1,0:T(8,128)} copy(f32[2,512,128]{2,1,0:T(8,128)} %get-tuple-element.4) | data formatting | bytes 1048576
  155.7 0.0 copy-done
  155.7 0.7 copy.10
Async XLA Ops:
  153.7 1.9 %copy-start = (f32[2,128,128]{2,1,0:T(8,128)S(1)}, f32[2,128,128]{2,1,0:T(8,128)}, u32[]{:S(2)}) copy-start(f32[2,128,128]{2,1,0:T(8,128)} %get-tuple-element.5) | copy-start | bytes 393220

commit v3 on v2

v3 whole, which is shorter than its diff:
```python
import functools

import jax
import jax.numpy as jnp
from jax import lax
from jax.experimental import pallas as pl
from jax.experimental.pallas import tpu as pltpu
from jax.sharding import PartitionSpec as P

MESH = pl.DeviceIdType.MESH
F32, BF16 = jnp.float32, jnp.bfloat16
BLOCK = 256
ROWS, COLS = 512, 128


def split(value):
    high = value.astype(BF16)
    return high, (value - high.astype(F32)).astype(BF16)


def dot(a, b):
    return jnp.dot(a, b, preferred_element_type=F32)


def landed(ref, sem):
    pltpu.make_async_copy(ref, ref, sem).wait()


class Sends:
    def __init__(self):
        self.started, self.done = [], 0

    def __call__(self, src, dst, send_sem, recv_sem, device):
        copy = pltpu.make_async_remote_copy(
            src_ref=src, dst_ref=dst, send_sem=send_sem, recv_sem=recv_sem, device_id=device, device_id_type=MESH
        )
        copy.start()
        self.started.append(copy)

    def finish(self, upto=None):
        upto = len(self.started) if upto is None else upto
        while self.done < upto:
            self.started[self.done].wait_send()
            self.done += 1


class ReduceScatter:
    def __init__(self, send, part, slots, send_sem, recv_sem, up, down):
        self.send, self.part, self.slots = send, part, slots
        self.send_sem, self.recv_sem = send_sem, recv_sem
        self.to = (up, down)

    def hop(self, way, half, d):
        first = 4 if half == way else 3
        mine = self.part(d if way == 0 else 8 - d, half)
        if d < first:
            slot = self.slots(way, half, d)
            landed(slot, self.recv_sem.at[way, half, d])
            mine[...] = mine[...] + slot[...]
        self.send(
            mine,
            self.slots(way, half, d - 1),
            self.send_sem.at[way, half, d],
            self.recv_sem.at[way, half, d - 1],
            self.to[way],
        )

    def step(self, t):
        for way, half in ((0, 0), (1, 1), (0, 1), (1, 0)):
            first = 4 if half == way else 3
            if first - t >= 1:
                self.hop(way, half, first - t)

    def total(self, half):
        up, down = self.slots(0, half, 0), self.slots(1, half, 0)
        landed(up, self.recv_sem.at[0, half, 0])
        landed(down, self.recv_sem.at[1, half, 0])
        return self.part(0, half)[...] + up[...] + down[...]


GROUPS = 2
PIECE = ROWS // 8
PART = PIECE // GROUPS
TALL = ROWS // GROUPS
LAG = 2
UNITS = [
    (0, 0, 0), (0, 3, 0), (0, 1, 0), (0, 2, 0), (0, 0, 1), (0, 3, 1), (0, 1, 1), (1, 0, 0),
    (1, 3, 0), (1, 1, 0), (1, 2, 0), (1, 0, 1), (0, 2, 1), (1, 3, 1), (1, 1, 1), (1, 2, 1),
]
PLANE = [(a, b, c) for b in range(2) for a in (0, 3, 1, 2) for c in range(2)]
LINE = [(a, b) for b in range(8) for a in range(2)][1:]


class Ring:
    def __init__(self, send, terms, slots, send_sem, recv_sem, z, to):
        self.send, self.terms, self.slots = send, terms, slots
        self.send_sem, self.recv_sem, self.z, self.to = send_sem, recv_sem, z, to

    def step(self, t):
        d = 4 - t
        for way in range(2):
            mine = self.terms.at[(self.z + (d if way == 0 else 8 - d)) % 8]
            half = pl.ds(way * (PART // 2), PART // 2)
            target = self.slots.at[way, d - 1]
            if d == 4:
                mine, target = mine.at[half], target.at[half]
            else:
                slot, into = self.slots.at[way, d], mine
                if d == 3:
                    slot, into = slot.at[half], mine.at[half]
                landed(slot, self.recv_sem.at[way, d])
                into[...] = into[...] + slot[...]
            self.send(mine, target, self.send_sem.at[way, d], self.recv_sem.at[way, d - 1], self.to[way])

    def total(self):
        for way in range(2):
            landed(self.slots.at[way, 0], self.recv_sem.at[way, 0])
        return self.terms[self.z] + self.slots[0, 0] + self.slots[1, 0]


class Gather:
    def __init__(self, send, buf, high, low_part, place, devices, x_s, x_r, f_s, f_r, c_s, c_r):
        self.send, self.buf, self.high, self.low_part = send, buf, high, low_part
        self.x, self.yh, self.yl, self.c = place
        self.right, self.left, self.sibling = devices
        self.x_s, self.x_r, self.f_s, self.f_r, self.c_s, self.c_r = x_s, x_r, f_s, f_r, c_s, c_r

    def piece(self, steps, r, other=0):
        y = (self.yh + r // 2) % 2 * 2 + (self.yl + r % 2) % 2
        return self.buf.at[(self.x + steps) % 4 * 2 + (self.c + other) % 2, y]

    def spread(self, r):
        piece = self.piece(0, r)
        self.send(piece, piece, self.x_s.at[0, r], self.x_r.at[0, r], self.right)
        self.send(piece, piece, self.x_s.at[1, r], self.x_r.at[1, r], self.left)
        self.share(0, r)

    def share(self, steps, r):
        piece = self.piece(steps, r)
        self.send(piece, piece, self.c_s.at[steps, r], self.c_r.at[steps, r], self.sibling)

    def neighbours(self, r):
        for side, steps, onward, forward in ((0, 3, self.right, (0, 3)), (1, 1, self.left, (1, 2))):
            piece = self.piece(steps, r)
            landed(piece, self.x_r.at[side, r])
            if r in forward:
                self.send(piece, piece, self.f_s.at[r], self.f_r.at[r], onward)
            self.share(steps, r)

    def opposite(self, r):
        landed(self.piece(2, r), self.f_r.at[r])
        self.share(2, r)

    def prepare(self, steps, turn):
        a, b = (self.x + steps) % 4, (self.yh + turn) % 2
        for r in (2 * turn, 2 * turn + 1):
            landed(self.piece(steps, r, 1), self.c_r.at[steps, r])
        for q in range(2):
            for k in range(2):
                high, low_part = split(self.buf[a * 2 + q, b * 2 + k])
                block = (a * 2 + b, pl.ds(k * ROWS, ROWS), pl.ds(q * COLS, COLS))
                self.high[block] = high
                self.low_part[block] = low_part


def kernel(
    s_ref, p_ref, anc, pat, d_ref, oij, ojj,
    pm, sm, sr, sh, sl, pall, ph, pln, pq, pall2, ph2, pln2, cp, zr, cf, cb, xo, lhs, ot, orr, fin, fr,
    y_s, y_r, s_s, s_r, x_s, x_r, f_s, f_r, c_s, c_r, z_s, z_r, b_s, b_r, e_s, e_r, o_s, o_r, h_s, h_r,
    q_s, q_r, y2_s, y2_r, x2_s, x2_r, f2_s, f2_r, c2_s, c2_r,
):
    brow, bcol = lax.axis_index("brow"), lax.axis_index("bcol")
    x, yh, c = brow // 4, brow // 2 % 2, brow % 2
    yl, z = bcol // 8, bcol % 8
    y = yh * 2 + yl
    own = x * 2 + c
    low = brow % 8
    diagonal = brow == bcol

    def at(x, y, z, c):
        return (x * 4 + (y // 2) * 2 + c, (y % 2) * 8 + z)

    def across_y(r):
        return (yh + r // 2) % 2 * 2 + (yl + r % 2) % 2

    def row(a, b, c_steps):
        return (x + a) % 4 * 4 + (yh + b) % 2 * 2 + (c + c_steps) % 2

    def column(a, b):
        return (yl + a) % 2 * 8 + (z + b) % 8

    right, left = at((x + 1) % 4, y, z, c), at((x + 3) % 4, y, z, c)
    up, down = at(x, y, (z + 1) % 8, c), at(x, y, (z + 7) % 8, c)
    sibling = at(x, y, z, 1 - c)
    partner = (brow, (1 - yl) * 8 + z)
    send = Sends()

    barrier = pltpu.get_barrier_semaphore()

    def greet(device):
        pl.semaphore_signal(barrier, inc=1, device_id=device, device_id_type=MESH)

    for steps in PLANE[1:]:
        greet((row(*steps), bcol))
    for steps in LINE:
        greet((brow, column(*steps)))
    greet(at(x, across_y(3), z, c))
    for k in range(2):
        pl.when(jnp.logical_or(brow != bcol, brow // 8 != k))(lambda k=k: greet((bcol, k * 8 + low)))

    for half in range(2):
        rows = pl.ds(half * BLOCK, BLOCK)
        pall[own, y, rows, :] = p_ref[yl, rows, :] * anc[yl, 2 * bcol + half].astype(F32)
        pm[rows, :] = p_ref[1 - yl, rows, :] * anc[1 - yl, 2 * bcol + half].astype(F32)

    pl.semaphore_wait(barrier, 33 - jnp.where(diagonal, 1, 0))

    def to_y(r):
        source = pm if r % 2 else pall.at[own, y]
        send(source, pall.at[own, y], y_s.at[r], y_r.at[r], at(x, across_y(r), z, c))

    devices = (right, left, sibling)
    one = Gather(send, pall, ph, pln, (x, yh, yl, c), devices, x_s, x_r, f_s, f_r, c_s, c_r)
    two = Gather(send, pall2, ph2, pln2, (x, yh, yl, c), devices, x2_s, x2_r, f2_s, f2_r, c2_s, c2_r)

    def from_y(r):
        landed(pall.at[own, across_y(r)], y_r.at[r])
        one.spread(r)

    def rows_of(step):
        return pl.ds(pl.multiple_of((z + step) % 8 * PIECE, PIECE), PIECE)

    def scatter():
        for step in range(1, 8):
            device = (brow, yl * 8 + (z + step) % 8)
            send(pall.at[own, y, rows_of(step)], pall2.at[own, y, rows_of(0)], q_s.at[0, step], q_r.at[0, step], device)
            send(pm.at[rows_of(step)], pq.at[rows_of(0)], q_s.at[1, step], q_r.at[1, step], device)
        pall2[own, y, rows_of(0), :] = pall[own, y, rows_of(0), :]
        pq[rows_of(0), :] = pm[rows_of(0), :]

    def scattered():
        for step in range(1, 8):
            landed(pall2.at[own, y, rows_of(8 - step)], q_r.at[0, step])
            landed(pq.at[rows_of(8 - step)], q_r.at[1, step])

    def to_y2(r):
        source = pq if r == 1 else pall2.at[own, across_y(r - 2)]
        target = y if r == 1 else across_y(r - 2)
        send(source, pall2.at[own, target], y2_s.at[r], y2_r.at[r], at(x, across_y(1 if r == 1 else 2), z, c))

    def from_y2(r):
        landed(pall2.at[own, across_y(r)], y2_r.at[r])
        two.spread(r)

    def swap(g):
        send(sm.at[g], sr.at[g], s_s.at[g], s_r.at[g], partner)

    to_y(1)
    to_y(3)
    one.spread(0)
    scatter()

    for g in range(GROUPS):
        for p in range(8):
            for k in range(2):
                columns = pl.ds(k * BLOCK, BLOCK)
                sm[g, pl.ds(p * PART, PART), columns] = (
                    s_ref[pl.ds(p * PIECE + g * PART, PART), columns] * pat[p // 4, k].astype(F32)
                )

    def place(g, value, index):
        high, low_part = split(value)
        for k in range(2):
            @pl.when(index == k)
            def _():
                sh[g, :, pl.ds(k * ROWS, ROWS)] = high
                sl[g, :, pl.ds(k * ROWS, ROWS)] = low_part

    def swapped(g):
        landed(sr.at[g], s_r.at[g])
        place(g, sr[g], 1 - yl)

    def multiply(n):
        g, steps, turn = UNITS[n]
        v = (x + steps) % 4 * 2 + (yh + turn) % 2
        a, b, value = sh[g], sl[g], ph[v]
        got = dot(a, pln[v]) + dot(b, value) + dot(a, value)
        cp[n] = got.reshape(8, PART, 2 * COLS)

    rings = [
        Ring(send, cp.at[n], zr.at[n], z_s.at[n], z_r.at[n], z, (up, down)) for n in range(len(UNITS))
    ]
    keep = -anc[yl, 2 * brow + z // 4].astype(F32)

    def finish(n):
        g, steps, turn = UNITS[n]
        total = rings[n].total() * keep
        for q in range(2):
            j = (x + steps) % 4 * 4 + (yh + turn) % 2 * 2 + q
            cf[j, pl.ds(g * PART, PART), :] = total[:, q * COLS : (q + 1) * COLS]
        if g == GROUPS - 1:
            for index, (a, b, d) in enumerate(PLANE):
                if (a, b) == (steps, turn) and index:
                    j = row(a, b, d)
                    send(cf.at[j], cb.at[brow], b_s.at[index], b_r.at[index], (j, bcol))

    def source(a, b, d):
        return row((4 - a) % 4, b, d)

    def out(first, last):
        for index in range(first, min(last, len(LINE))):
            a, b = LINE[index]
            send(cf.at[column(a, b)], xo.at[yl, z], e_s.at[index], e_r.at[index], (brow, column(a, b)))

    for g in range(GROUPS):
        place(g, sm[g], yl)
    from_y(1)
    swap(0)
    one.neighbours(0)
    from_y(3)
    one.neighbours(1)
    marks = []
    for time in range(len(UNITS) + 4 * LAG):
        for t in (3, 2, 1):
            if 0 <= time - t * LAG < len(UNITS):
                rings[time - t * LAG].step(t)
        if time == 0:
            swapped(0)
            to_y(2)
        if time == 1:
            scattered()
        if time == 3:
            from_y(2)
            swap(1)
            one.opposite(0)
            one.opposite(1)
        if time == 4:
            one.neighbours(3)
            two.spread(0)
        if time == 5:
            one.neighbours(2)
        if time == 7:
            swapped(1)
            to_y2(1)
            to_y2(2)
        if time == 9:
            two.neighbours(0)
        if time == 10:
            from_y2(1)
            to_y2(3)
        if time == 12:
            one.opposite(3)
            one.opposite(2)
            from_y2(2)
        if time == 14:
            two.prepare(0, 0)
            from_y2(3)
        if time == 16:
            two.neighbours(1)
            two.prepare(3, 0)
            two.prepare(1, 0)
        if time == 18:
            two.neighbours(2)
            two.prepare(0, 1)
        if time == 21:
            two.neighbours(3)
        if time == 22:
            two.prepare(3, 1)
        if time == 23:
            two.prepare(1, 1)
        if time < len(UNITS):
            g, steps, turn = UNITS[time]
            if g == 0:
                one.prepare(steps, turn)
            multiply(time)
            rings[time].step(0)
        if time >= 4 * LAG:
            finish(time - 4 * LAG)
        marks.append(len(send.started))
        if time >= 8:
            send.finish(marks[time - 8])
    cb[brow] = cf[brow]
    out(0, 15)
    for r in range(4):
        two.opposite(r)
    for index, steps in enumerate(PLANE[1:], 1):
        landed(cb.at[source(*steps)], b_r.at[index])

    turned = jnp.concatenate([cb[pl.ds(k * 8, 8)].reshape(ROWS, COLS).T for k in range(2)], axis=1)
    high, low_part = split(turned)
    lhs[pl.ds(0, COLS), :] = high
    lhs[pl.ds(COLS, COLS), :] = low_part

    def unit(v, carry):
        value = ph2[v]
        got = dot(lhs[...], value)
        got = got[:COLS] + got[COLS:] + dot(lhs[pl.ds(0, COLS), :], pln2[v])
        for q in range(2):
            ot[v * 2 + q] = got[:, q * COLS : (q + 1) * COLS]
        return carry

    two.prepare(2, 0)
    two.prepare(2, 1)
    lax.fori_loop(0, 8, unit, 0)
    last = ReduceScatter(
        send,
        lambda d, half: ot.at[half * 8 + (z + d) % 8],
        lambda way, half, d: orr.at[way, half, d],
        o_s, o_r, up, down,
    )
    for t in range(4):
        last.step(t)
        if t == 0:
            send.finish(marks[-4])
    xo[yl, z] = cf[bcol]

    def home(h):
        return pltpu.make_async_remote_copy(
            src_ref=fin.at[h], dst_ref=fr.at[yl], send_sem=h_s.at[h], recv_sem=h_r.at[yl],
            device_id=(z + 8 * h, brow), device_id_type=MESH,
        )

    def away(h):
        return jnp.logical_or(jnp.logical_not(diagonal), yl != h)

    for h in range(2):
        fin[h] = last.total(h)
        pl.when(away(h))(lambda h=h: home(h).start())
    for index, (a, b) in enumerate(LINE):
        landed(xo.at[(yl + a) % 2, (z + 8 - b) % 8], e_r.at[index])
    oij[...] = xo[...].reshape(2, ROWS, COLS)

    @pl.when(diagonal)
    def _():
        fr[yl] = fin[yl]

    for k in range(2):
        pl.when(jnp.logical_or(brow != bcol, brow // 8 != k))(lambda k=k: landed(fr.at[k], h_r.at[k]))
        ojj[k] = d_ref[k] - fr[k].T

    for h in range(2):
        pl.when(away(h))(lambda h=h: home(h).wait_send())
    send.finish()


def on_device(inverse_block, panels, ancestor_blocks, pattern, diag_inverse):
    vmem, smem = pl.BlockSpec(memory_space=pltpu.VMEM), pl.BlockSpec(memory_space=pltpu.SMEM)
    dma = pltpu.SemaphoreType.DMA
    count = len(UNITS)
    semaphores = [
        (4,), (GROUPS,), (2, 4), (4,), (4, 4), (count, 2, 5), (16,), (15,), (2, 2, 5), (2,), (2, 8), (4,), (2, 4), (4,), (4, 4)
    ]
    return pl.pallas_call(
        kernel,
        out_shape=(
            jax.ShapeDtypeStruct((2, ROWS, COLS), F32),
            jax.ShapeDtypeStruct((2, COLS, COLS), F32),
        ),
        in_specs=[vmem, vmem, smem, smem, vmem],
        out_specs=(vmem, vmem),
        scratch_shapes=[
            pltpu.VMEM((ROWS, COLS), F32),
            pltpu.VMEM((GROUPS, TALL, ROWS), F32),
            pltpu.VMEM((GROUPS, TALL, ROWS), F32),
            pltpu.VMEM((GROUPS, TALL, 2 * ROWS), BF16),
            pltpu.VMEM((GROUPS, TALL, 2 * ROWS), BF16),
            pltpu.VMEM((8, 4, ROWS, COLS), F32),
            pltpu.VMEM((8, 2 * ROWS, 2 * COLS), BF16),
            pltpu.VMEM((8, 2 * ROWS, 2 * COLS), BF16),
            pltpu.VMEM((ROWS, COLS), F32),
            pltpu.VMEM((8, 4, ROWS, COLS), F32),
            pltpu.VMEM((8, 2 * ROWS, 2 * COLS), BF16),
            pltpu.VMEM((8, 2 * ROWS, 2 * COLS), BF16),
            pltpu.VMEM((count, 8, PART, 2 * COLS), F32),
            pltpu.VMEM((count, 2, 4, PART, 2 * COLS), F32),
            pltpu.VMEM((16, PIECE, COLS), F32),
            pltpu.VMEM((16, PIECE, COLS), F32),
            pltpu.VMEM((2, 8, PIECE, COLS), F32),
            pltpu.VMEM((2 * COLS, 2 * ROWS), BF16),
            pltpu.VMEM((16, COLS, COLS), F32),
            pltpu.VMEM((2, 2, 4, COLS, COLS), F32),
            pltpu.VMEM((2, COLS, COLS), F32),
            pltpu.VMEM((2, COLS, COLS), F32),
        ]
        + [dma(shape) for shape in semaphores for _ in range(2)],
        compiler_params=pltpu.CompilerParams(
            collective_id=0, has_side_effects=True, vmem_limit_bytes=60 * 2**20
        ),
        cost_estimate=pl.CostEstimate(flops=8 * 10**9, bytes_accessed=3 * 2**20, transcendentals=0),
        name="selected_inverse",
    )(inverse_block, panels, ancestor_blocks, pattern, diag_inverse)


def solution(mesh):
    return jax.shard_map(
        on_device,
        mesh=mesh,
        in_specs=(
            P("brow", "bcol"),
            P(None, "bcol", "brow"),
            P(),
            P("brow", "bcol"),
            P(None, "brow", "bcol"),
        ),
        out_specs=(P(None, "brow", "bcol"), P(None, "brow", "bcol")),
        check_vma=False,
    )
```

time: 156 us -> 137 us (0.88)
  Pallas kernels: 153 us -> 134 us
    pallas_call x1, Pallas kernels: 153 us -> 134 us  [on_device(): pl.pallas_call(kernel, out_shape=(jax.ShapeDtypeStruct((2, ROWS, COLS), F...]
where the time goes in v3:
time: 137 us
  Pallas kernels  134 us (98%)
  local copies, waits for them, and re-layouts  2.56 us (2%)
    pallas_call x1, Pallas kernels, on_device(): pl.pallas_call(kernel, out_shape=(jax.ShapeDtypeStruct((2, ROWS, COLS), F...  134 us

profile of v3, /device:TPU:5, one launch (start us, length us, event | category | flops | bytes accessed | tf_op | source)
XLA Modules:
  0.0 137.0 jit_solution(9403884663609631873)
XLA Ops:
  0.6 133.8 %selected_inverse.1 = (f32[2,512,128]{2,1,0:T(8,128)}, f32[2,128,128]{2,1,0:T(8,128)}) custom-call(f32[512,512]{1,0:T(8,128)} %s_ref.1, f32[2,512,128]{2,1,0:T(8,128)} %p_ref.1, s32[2,32]{1,0:T(2,128)} %anc.1, s32[2,2]{1,0:T(2,128)} %pat.1, f32[2,128,128]{2,1,0:T(8,128)} %d_ref.1), custom_call_target="tpu_custom_call" | custom-call | flops 8000000000 | bytes 3145728 | tf_op jit(solution)/shard_map/selected_inverse/pallas_call | solution.py:453
  134.5 0.0 copy-start
  134.5 1.9 %copy.9 = f32[2,512,128]{2,1,0:T(8,128)} copy(f32[2,512,128]{2,1,0:T(8,128)} %get-tuple-element.4) | data formatting | bytes 1048576
  136.4 0.0 copy-done
  136.4 0.7 copy.10
Async XLA Ops:
  134.5 1.9 %copy-start = (f32[2,128,128]{2,1,0:T(8,128)S(1)}, f32[2,128,128]{2,1,0:T(8,128)}, u32[]{:S(2)}) copy-start(f32[2,128,128]{2,1,0:T(8,128)} %get-tuple-element.5) | copy-start | bytes 393220

commit v4 on v3

v4 whole, which is shorter than its diff:
```python
import functools

import jax
import jax.numpy as jnp
from jax import lax
from jax.experimental import pallas as pl
from jax.experimental.pallas import tpu as pltpu
from jax.sharding import PartitionSpec as P

MESH = pl.DeviceIdType.MESH
F32, BF16 = jnp.float32, jnp.bfloat16
BLOCK = 256
ROWS, COLS = 512, 128


def split(value):
    high = value.astype(BF16)
    return high, (value - high.astype(F32)).astype(BF16)


def dot(a, b):
    return jnp.dot(a, b, preferred_element_type=F32)


def landed(ref, sem):
    pltpu.make_async_copy(ref, ref, sem).wait()


def send(src, dst, send_sem, recv_sem, device):
    pltpu.make_async_remote_copy(
        src_ref=src, dst_ref=dst, send_sem=send_sem, recv_sem=recv_sem, device_id=device, device_id_type=MESH
    ).start()


class ReduceScatter:
    def __init__(self, part, slots, send_sem, recv_sem, up, down):
        self.part, self.slots = part, slots
        self.send_sem, self.recv_sem = send_sem, recv_sem
        self.to = (up, down)

    def hop(self, way, half, d):
        first = 4 if half == way else 3
        mine = self.part(d if way == 0 else 8 - d, half)
        if d < first:
            slot = self.slots(way, half, d)
            landed(slot, self.recv_sem.at[way, half, d])
            mine[...] = mine[...] + slot[...]
        send(
            mine,
            self.slots(way, half, d - 1),
            self.send_sem,
            self.recv_sem.at[way, half, d - 1],
            self.to[way],
        )

    def step(self, t):
        for way, half in ((0, 0), (1, 1), (0, 1), (1, 0)):
            first = 4 if half == way else 3
            if first - t >= 1:
                self.hop(way, half, first - t)

    def total(self, half):
        up, down = self.slots(0, half, 0), self.slots(1, half, 0)
        landed(up, self.recv_sem.at[0, half, 0])
        landed(down, self.recv_sem.at[1, half, 0])
        return self.part(0, half)[...] + up[...] + down[...]


GROUPS = 2
PIECE = ROWS // 8
PART = PIECE // GROUPS
TALL = ROWS // GROUPS
LAG = 2
UNITS = [
    (0, 0, 0), (0, 3, 0), (0, 1, 0), (0, 2, 0), (0, 0, 1), (0, 3, 1), (0, 1, 1), (1, 0, 0),
    (1, 3, 0), (1, 1, 0), (1, 2, 0), (1, 0, 1), (0, 2, 1), (1, 3, 1), (1, 1, 1), (1, 2, 1),
]
PLANE = [(a, b, c) for b in range(2) for a in (0, 3, 1, 2) for c in range(2)]
LINE = [(a, b) for b in range(8) for a in range(2)][1:]


class Ring:
    def __init__(self, terms, slots, send_sem, recv_sem, z, to):
        self.terms, self.slots = terms, slots
        self.send_sem, self.recv_sem, self.z, self.to = send_sem, recv_sem, z, to

    def step(self, t):
        d = 4 - t
        for way in range(2):
            mine = self.terms.at[(self.z + (d if way == 0 else 8 - d)) % 8]
            half = pl.ds(way * (PART // 2), PART // 2)
            target = self.slots.at[way, d - 1]
            if d == 4:
                mine, target = mine.at[half], target.at[half]
            else:
                slot, into = self.slots.at[way, d], mine
                if d == 3:
                    slot, into = slot.at[half], mine.at[half]
                landed(slot, self.recv_sem.at[way, d])
                into[...] = into[...] + slot[...]
            send(mine, target, self.send_sem, self.recv_sem.at[way, d - 1], self.to[way])

    def total(self):
        for way in range(2):
            landed(self.slots.at[way, 0], self.recv_sem.at[way, 0])
        return self.terms[self.z] + self.slots[0, 0] + self.slots[1, 0]


class Gather:
    def __init__(self, buf, high, low_part, turns, place, devices, x_s, x_r, f_s, f_r, c_s, c_r):
        self.buf, self.high, self.low_part, self.turns = buf, high, low_part, turns
        self.x, self.yh, self.yl, self.c = place
        self.right, self.left, self.sibling = devices
        self.x_s, self.x_r, self.f_s, self.f_r, self.c_s, self.c_r = x_s, x_r, f_s, f_r, c_s, c_r

    def piece(self, steps, r, other=0):
        block = (self.yh + r // 2) % self.turns * 2 + (self.yl + r % 2) % 2
        return self.buf.at[(self.x + steps) % 4 * 2 + (self.c + other) % 2, block]

    def spread(self, r):
        piece = self.piece(0, r)
        send(piece, piece, self.x_s, self.x_r.at[0, r], self.right)
        send(piece, piece, self.x_s, self.x_r.at[1, r], self.left)
        self.share(0, r)

    def share(self, steps, r):
        piece = self.piece(steps, r)
        send(piece, piece, self.c_s, self.c_r.at[steps, r // 2], self.sibling)

    def neighbours(self, r):
        for side, steps, onward, forward in ((0, 3, self.right, (0, 3)), (1, 1, self.left, (1, 2))):
            piece = self.piece(steps, r)
            landed(piece, self.x_r.at[side, r])
            if r in forward:
                send(piece, piece, self.f_s, self.f_r.at[r], onward)
            self.share(steps, r)

    def opposite(self, r):
        landed(self.piece(2, r), self.f_r.at[r])
        self.share(2, r)

    def prepare(self, steps, turn):
        a, b = (self.x + steps) % 4, (self.yh + turn) % self.turns
        landed(self.buf.at[a * 2 + 1 - self.c, pl.ds(b * 2, 2)], self.c_r.at[steps, turn])
        for q in range(2):
            for k in range(2):
                high, low_part = split(self.buf[a * 2 + q, b * 2 + k])
                block = (a * self.turns + b, pl.ds(k * ROWS, ROWS), pl.ds(q * COLS, COLS))
                self.high[block] = high
                self.low_part[block] = low_part


def kernel(
    s_ref, p_ref, anc, pat, d_ref, oij, ojj,
    pm, sm, sr, sh, sl, pall, ph, pln, pq, pall2, ph2, pln2, cp, zr, cf, cb, xo, lhs, ot, orr, fin, fr,
    y_s, y_r, s_s, s_r, x_s, x_r, f_s, f_r, c_s, c_r, z_s, z_r, b_s, b_r, e_s, e_r, o_s, o_r, h_s, h_r,
    q_s, q_r, y2_s, y2_r, x2_s, x2_r, f2_s, f2_r, c2_s, c2_r,
):
    brow, bcol = lax.axis_index("brow"), lax.axis_index("bcol")
    x, yh, c = brow // 4, brow // 2 % 2, brow % 2
    yl, z = bcol // 8, bcol % 8
    y = yh * 2 + yl
    own = x * 2 + c

    def from_afar(k):
        return jnp.logical_or(bcol // 4 * 4 + yh * 2 + bcol % 2 != brow, k * 8 + x * 2 + c != bcol)


    def at(x, y, z, c):
        return (x * 4 + (y // 2) * 2 + c, (y % 2) * 8 + z)

    def across_y(r):
        return (yh + r // 2) % 2 * 2 + (yl + r % 2) % 2

    def row(a, b, c_steps):
        return (x + a) % 4 * 4 + (yh + b) % 2 * 2 + (c + c_steps) % 2

    def column(a, b):
        return (yl + a) % 2 * 8 + (z + b) % 8

    right, left = at((x + 1) % 4, y, z, c), at((x + 3) % 4, y, z, c)
    up, down = at(x, y, (z + 1) % 8, c), at(x, y, (z + 7) % 8, c)
    sibling = at(x, y, z, 1 - c)
    partner = (brow, (1 - yl) * 8 + z)

    barrier = pltpu.get_barrier_semaphore()

    def greet(device):
        pl.semaphore_signal(barrier, inc=1, device_id=device, device_id_type=MESH)

    for steps in PLANE[1:]:
        greet((row(*steps), bcol))
    for steps in LINE:
        greet((brow, column(*steps)))
    greet(at(x, across_y(3), z, c))
    for k in range(2):
        pl.when(from_afar(k))(lambda k=k: greet((bcol // 4 * 4 + yh * 2 + bcol % 2, k * 8 + x * 2 + c)))

    for half in range(2):
        rows = pl.ds(half * BLOCK, BLOCK)
        pall[own, y, rows, :] = p_ref[yl, rows, :] * anc[yl, 2 * bcol + half].astype(F32)
        pm[rows, :] = p_ref[1 - yl, rows, :] * anc[1 - yl, 2 * bcol + half].astype(F32)

    pl.semaphore_wait(barrier, 31 + sum(jnp.where(from_afar(k), 1, 0) for k in range(2)))

    def to_y(r):
        source = pm if r % 2 else pall.at[own, y]
        send(source, pall.at[own, y], y_s.at[r], y_r.at[r], at(x, across_y(r), z, c))

    devices = (right, left, sibling)
    one = Gather(pall, ph, pln, 2, (x, yh, yl, c), devices, x_s, x_r, f_s, f_r, c_s, c_r)
    two = Gather(pall2, ph2, pln2, 1, (x, yh, yl, c), devices, x2_s, x2_r, f2_s, f2_r, c2_s, c2_r)

    def from_y(r):
        landed(pall.at[own, across_y(r)], y_r.at[r])
        one.spread(r)

    def rows_of(step):
        return pl.ds(pl.multiple_of((z + step) % 8 * PIECE, PIECE), PIECE)

    def scatter():
        for step in range(1, 8):
            device = (brow, yl * 8 + (z + step) % 8)
            send(pall.at[own, y, rows_of(step)], pall2.at[own, yl, rows_of(0)], q_s, q_r.at[0], device)
            send(pm.at[rows_of(step)], pq.at[rows_of(0)], q_s, q_r.at[1], device)
        pall2[own, yl, rows_of(0), :] = pall[own, y, rows_of(0), :]
        pq[rows_of(0), :] = pm[rows_of(0), :]

    def scattered():
        landed(pall2.at[own, yl, pl.ds(0, 7 * PIECE)], q_r.at[0])
        landed(pq.at[pl.ds(0, 7 * PIECE)], q_r.at[1])

    def exchange():
        send(pq, pall2.at[own, yl], y2_s, y2_r, partner)

    def exchanged():
        landed(pall2.at[own, 1 - yl], y2_r)
        two.spread(1)

    def swap(g):
        send(sm.at[g], sr.at[g], s_s.at[g], s_r.at[g], partner)

    to_y(1)
    to_y(3)
    one.spread(0)
    scatter()

    for g in range(GROUPS):
        for p in range(8):
            for k in range(2):
                columns = pl.ds(k * BLOCK, BLOCK)
                sm[g, pl.ds(p * PART, PART), columns] = (
                    s_ref[pl.ds(p * PIECE + g * PART, PART), columns] * pat[p // 4, k].astype(F32)
                )

    def place(g, value, index):
        high, low_part = split(value)
        for k in range(2):
            @pl.when(index == k)
            def _():
                sh[g, :, pl.ds(k * ROWS, ROWS)] = high
                sl[g, :, pl.ds(k * ROWS, ROWS)] = low_part

    def swapped(g):
        landed(sr.at[g], s_r.at[g])
        place(g, sr[g], 1 - yl)

    def multiply(n):
        g, steps, turn = UNITS[n]
        v = (x + steps) % 4 * 2 + (yh + turn) % 2
        a, b, value = sh[g], sl[g], ph[v]
        got = dot(a, pln[v]) + dot(b, value) + dot(a, value)
        cp[n] = got.reshape(8, PART, 2 * COLS)

    rings = [
        Ring(cp.at[n], zr.at[n], z_s.at[n], z_r.at[n], z, (up, down)) for n in range(len(UNITS))
    ]
    keep = -anc[yl, 2 * brow + z // 4].astype(F32)

    def finish(n):
        g, steps, turn = UNITS[n]
        total = rings[n].total() * keep
        for q in range(2):
            j = (x + steps) % 4 * 4 + (yh + turn) % 2 * 2 + q
            cf[j, pl.ds(g * PART, PART), :] = total[:, q * COLS : (q + 1) * COLS]
        if g == GROUPS - 1:
            for a, b, d in PLANE[1:]:
                if a == steps:
                    source, target = cf.at[row(a, turn, d)], cb.at[(yh + turn) % 2, brow]
                    send(source, target, b_s, b_r, (row(a, b, d), bcol))

    def out():
        for a, b in LINE:
            send(cf.at[column(a, b)], xo.at[yl, z], e_s, e_r.at[a], (brow, column(a, b)))

    for g in range(GROUPS):
        place(g, sm[g], yl)
    from_y(1)
    swap(0)
    one.neighbours(0)
    from_y(3)
    one.neighbours(1)
    for time in range(len(UNITS) + 4 * LAG):
        for t in (3, 2, 1):
            if 0 <= time - t * LAG < len(UNITS):
                rings[time - t * LAG].step(t)
        if time == 0:
            swapped(0)
            to_y(2)
        if time == 1:
            scattered()
        if time == 3:
            from_y(2)
            swap(1)
            one.opposite(0)
            one.opposite(1)
        if time == 4:
            one.neighbours(3)
            two.spread(0)
        if time == 5:
            one.neighbours(2)
        if time == 7:
            swapped(1)
            exchange()
        if time == 9:
            two.neighbours(0)
        if time == 11:
            exchanged()
        if time == 12:
            one.opposite(3)
            one.opposite(2)
        if time == 16:
            two.neighbours(1)
        if time == 17:
            two.opposite(0)
        if time == 18:
            two.prepare(0, 0)
        if time == 19:
            two.prepare(3, 0)
        if time == 20:
            two.opposite(1)
            two.prepare(1, 0)
        if time == 21:
            two.prepare(2, 0)
        if time < len(UNITS):
            g, steps, turn = UNITS[time]
            if g == 0:
                one.prepare(steps, turn)
            multiply(time)
            rings[time].step(0)
        if time >= 4 * LAG:
            finish(time - 4 * LAG)
    for turn in range(2):
        cb[(yh + turn) % 2, brow] = cf[row(0, turn, 0)]
    out()
    landed(cb.at[:, pl.ds(0, 15)], b_r)

    for k in range(2):
        for half in range(2):
            high, low_part = split(cb[k, pl.ds(half * 8, 8)].reshape(ROWS, COLS).T)
            lhs[0, pl.ds(k * COLS, COLS), pl.ds(half * ROWS, ROWS)] = high
            lhs[1, pl.ds(k * COLS, COLS), pl.ds(half * ROWS, ROWS)] = low_part

    def unit(v, carry):
        a, b, value = lhs[0], lhs[1], ph2[v]
        got = dot(a, pln2[v]) + dot(b, value) + dot(a, value)
        for k in range(2):
            for q in range(2):
                ot[k, v * 2 + q] = got[k * COLS : (k + 1) * COLS, q * COLS : (q + 1) * COLS]
        return carry

    lax.fori_loop(0, 4, unit, 0)
    last = ReduceScatter(
        lambda d, half: ot.at[half, (z + d) % 8],
        lambda way, half, d: orr.at[way, half, d],
        o_s, o_r, up, down,
    )
    for t in range(4):
        last.step(t)
    xo[yl, z] = cf[bcol]

    def home(h):
        return pltpu.make_async_remote_copy(
            src_ref=fin.at[h], dst_ref=fr.at[yl], send_sem=h_s.at[h], recv_sem=h_r.at[yl],
            device_id=(z // 2 * 4 + yh * 2 + z % 2, x * 4 + h * 2 + c), device_id_type=MESH,
        )

    def away(h):
        return jnp.logical_or(z != x * 2 + c, bcol != x * 4 + h * 2 + c)

    for h in range(2):
        fin[h] = last.total(h)
        pl.when(away(h))(lambda h=h: home(h).start())
    landed(xo.at[yl, pl.ds(0, 7)], e_r.at[0])
    landed(xo.at[1 - yl], e_r.at[1])
    oij[...] = xo[...].reshape(2, ROWS, COLS)

    for h in range(2):
        @pl.when(jnp.logical_not(away(h)))
        def _():
            fr[yl] = fin[h]

    for k in range(2):
        pl.when(from_afar(k))(lambda k=k: landed(fr.at[k], h_r.at[k]))
        ojj[k] = d_ref[k] - fr[k].T

    for h in range(2):
        pl.when(away(h))(lambda h=h: home(h).wait_send())
    for r in (1, 2, 3):
        landed(pm, y_s.at[r])
    for g in range(GROUPS):
        landed(sm.at[g], s_s.at[g])
    landed(pq, y2_s)
    landed(pall.at[pl.ds(0, 2)], x_s)
    landed(pall.at[0], f_s)
    landed(pall.at[pl.ds(0, 4)], c_s)
    landed(pall2.at[pl.ds(0, 2)], x2_s)
    landed(pall2.at[0], f2_s)
    landed(pall2.at[pl.ds(0, 4)], c2_s)
    for n in range(len(UNITS)):
        landed(cp.at[n, pl.ds(0, 7)], z_s.at[n])
    landed(cb.at[:, pl.ds(0, 15)], b_s)
    landed(cf.at[pl.ds(0, 15)], e_s)
    landed(cf.at[pl.ds(0, 14)], q_s)
    landed(ot.at[:, pl.ds(0, 7)], o_s)


def on_device(inverse_block, panels, ancestor_blocks, pattern, diag_inverse):
    vmem, smem = pl.BlockSpec(memory_space=pltpu.VMEM), pl.BlockSpec(memory_space=pltpu.SMEM)
    dma = pltpu.SemaphoreType.DMA
    count = len(UNITS)
    semaphores = [
        (4,), (4,), (GROUPS,), (GROUPS,), (), (2, 4), (), (4,), (), (4, 2), (count,), (count, 2, 4), (), (), (), (2,),
        (), (2, 2, 4), (2,), (2,), (), (2,), (), (), (), (2, 2), (), (2,), (), (4, 1),
    ]
    return pl.pallas_call(
        kernel,
        out_shape=(
            jax.ShapeDtypeStruct((2, ROWS, COLS), F32),
            jax.ShapeDtypeStruct((2, COLS, COLS), F32),
        ),
        in_specs=[vmem, vmem, smem, smem, vmem],
        out_specs=(vmem, vmem),
        scratch_shapes=[
            pltpu.VMEM((ROWS, COLS), F32),
            pltpu.VMEM((GROUPS, TALL, ROWS), F32),
            pltpu.VMEM((GROUPS, TALL, ROWS), F32),
            pltpu.VMEM((GROUPS, TALL, 2 * ROWS), BF16),
            pltpu.VMEM((GROUPS, TALL, 2 * ROWS), BF16),
            pltpu.VMEM((8, 4, ROWS, COLS), F32),
            pltpu.VMEM((8, 2 * ROWS, 2 * COLS), BF16),
            pltpu.VMEM((8, 2 * ROWS, 2 * COLS), BF16),
            pltpu.VMEM((ROWS, COLS), F32),
            pltpu.VMEM((8, 2, ROWS, COLS), F32),
            pltpu.VMEM((4, 2 * ROWS, 2 * COLS), BF16),
            pltpu.VMEM((4, 2 * ROWS, 2 * COLS), BF16),
            pltpu.VMEM((count, 8, PART, 2 * COLS), F32),
            pltpu.VMEM((count, 2, 4, PART, 2 * COLS), F32),
            pltpu.VMEM((16, PIECE, COLS), F32),
            pltpu.VMEM((2, 16, PIECE, COLS), F32),
            pltpu.VMEM((2, 8, PIECE, COLS), F32),
            pltpu.VMEM((2, 2 * COLS, 2 * ROWS), BF16),
            pltpu.VMEM((2, 8, COLS, COLS), F32),
            pltpu.VMEM((2, 2, 4, COLS, COLS), F32),
            pltpu.VMEM((2, COLS, COLS), F32),
            pltpu.VMEM((2, COLS, COLS), F32),
        ]
        + [dma(shape) for shape in semaphores],
        compiler_params=pltpu.CompilerParams(
            collective_id=0, has_side_effects=True, vmem_limit_bytes=56 * 2**20
        ),
        cost_estimate=pl.CostEstimate(flops=8 * 10**9, bytes_accessed=3 * 2**20, transcendentals=0),
        name="selected_inverse",
    )(inverse_block, panels, ancestor_blocks, pattern, diag_inverse)


def solution(mesh):
    return jax.shard_map(
        on_device,
        mesh=mesh,
        in_specs=(
            P("brow", "bcol"),
            P(None, "bcol", "brow"),
            P(),
            P("brow", "bcol"),
            P(None, "brow", "bcol"),
        ),
        out_specs=(P(None, "brow", "bcol"), P(None, "brow", "bcol")),
        check_vma=False,
    )
```

time: 137 us -> 128 us (0.934); the launches traced: 137 us -> 126 us
  Pallas kernels: 134 us -> 123 us
    pallas_call x1, Pallas kernels: 134 us -> 123 us  [on_device(): pl.pallas_call(kernel, out_shape=(jax.ShapeDtypeStruct((2, ROWS, COLS), F...]
where the time goes in v4:
time: 128 us; the launch traced here: 126 us
  Pallas kernels  123 us (96%)
  local copies, waits for them, and re-layouts  2.56 us (2%)
    pallas_call x1, Pallas kernels, on_device(): pl.pallas_call(kernel, out_shape=(jax.ShapeDtypeStruct((2, ROWS, COLS), F...  123 us
    unnamed x4, local copies, waits for them, and re-layouts  2.56 us

profile of v4, /device:TPU:5, one launch (start us, length us, event | category | flops | bytes accessed | tf_op | source)
XLA Modules:
  0.0 126.0 jit_solution(4042810672830087634)
XLA Ops:
  0.6 122.8 %selected_inverse.1 = (f32[2,512,128]{2,1,0:T(8,128)}, f32[2,128,128]{2,1,0:T(8,128)}) custom-call(f32[512,512]{1,0:T(8,128)} %s_ref.1, f32[2,512,128]{2,1,0:T(8,128)} %p_ref.1, s32[2,32]{1,0:T(2,128)} %anc.1, s32[2,2]{1,0:T(2,128)} %pat.1, f32[2,128,128]{2,1,0:T(8,128)} %d_ref.1), custom_call_target="tpu_custom_call" | custom-call | flops 8000000000 | bytes 3145728 | tf_op jit(solution)/shard_map/selected_inverse/pallas_call | solution.py:436
  123.4 0.0 copy-start
  123.4 1.9 %copy.9 = f32[2,512,128]{2,1,0:T(8,128)} copy(f32[2,512,128]{2,1,0:T(8,128)} %get-tuple-element.4) | data formatting | bytes 1048576
  125.3 0.0 copy-done
  125.3 0.7 copy.10
Async XLA Ops:
  123.4 1.9 %copy-start = (f32[2,128,128]{2,1,0:T(8,128)S(1)}, f32[2,128,128]{2,1,0:T(8,128)}, u32[]{:S(2)}) copy-start(f32[2,128,128]{2,1,0:T(8,128)} %get-tuple-element.5) | copy-start | bytes 393220

commit v5 on v4

--- a/solution.py
+++ b/solution.py
@@ -75,6 +75,9 @@
     (0, 0, 0), (0, 3, 0), (0, 1, 0), (0, 2, 0), (0, 0, 1), (0, 3, 1), (0, 1, 1), (1, 0, 0),
     (1, 3, 0), (1, 1, 0), (1, 2, 0), (1, 0, 1), (0, 2, 1), (1, 3, 1), (1, 1, 1), (1, 2, 1),
 ]
+GROUPS_DONE = [unit[1:] for unit in UNITS if unit[0] == 1]
+OUT_TIME = [21, 22]
+OUT_LATER = len(OUT_TIME)
 PLANE = [(a, b, c) for b in range(2) for a in (0, 3, 1, 2) for c in range(2)]
 LINE = [(a, b) for b in range(8) for a in range(2)][1:]
 
@@ -151,7 +154,8 @@
 
 
 def kernel(
-    s_ref, p_ref, anc, pat, d_ref, oij, ojj,
+    s_hbm, p_hbm, anc, pat, oij, ojj,
+    s_ref, p_ref, in_sem,
     pm, sm, sr, sh, sl, pall, ph, pln, pq, pall2, ph2, pln2, cp, zr, cf, cb, xo, lhs, ot, orr, fin, fr,
     y_s, y_r, s_s, s_r, x_s, x_r, f_s, f_r, c_s, c_r, z_s, z_r, b_s, b_r, e_s, e_r, o_s, o_r, h_s, h_r,
     q_s, q_r, y2_s, y2_r, x2_s, x2_r, f2_s, f2_r, c2_s, c2_r,
@@ -183,6 +187,9 @@
     sibling = at(x, y, z, 1 - c)
     partner = (brow, (1 - yl) * 8 + z)
 
+    loads = [pltpu.make_async_copy(a, b, in_sem.at[k]) for k, (a, b) in enumerate(((p_hbm, p_ref), (s_hbm, s_ref)))]
+    for load in loads:
+        load.start()
     barrier = pltpu.get_barrier_semaphore()
 
     def greet(device):
@@ -196,6 +203,7 @@
     for k in range(2):
         pl.when(from_afar(k))(lambda k=k: greet((bcol // 4 * 4 + yh * 2 + bcol % 2, k * 8 + x * 2 + c)))
 
+    loads[0].wait()
     for half in range(2):
         rows = pl.ds(half * BLOCK, BLOCK)
         pall[own, y, rows, :] = p_ref[yl, rows, :] * anc[yl, 2 * bcol + half].astype(F32)
@@ -245,6 +253,7 @@
     one.spread(0)
     scatter()
 
+    loads[1].wait()
     for g in range(GROUPS):
         for p in range(8):
             for k in range(2):
@@ -275,7 +284,7 @@
     rings = [
         Ring(cp.at[n], zr.at[n], z_s.at[n], z_r.at[n], z, (up, down)) for n in range(len(UNITS))
     ]
-    keep = -anc[yl, 2 * brow + z // 4].astype(F32)
+    keep = anc[yl, 2 * brow + z // 4].astype(F32)
 
     def finish(n):
         g, steps, turn = UNITS[n]
@@ -289,9 +298,12 @@
                     source, target = cf.at[row(a, turn, d)], cb.at[(yh + turn) % 2, brow]
                     send(source, target, b_s, b_r, (row(a, b, d), bcol))
 
-    def out():
-        for a, b in LINE:
-            send(cf.at[column(a, b)], xo.at[yl, z], e_s, e_r.at[a], (brow, column(a, b)))
+    def out(steps, turn):
+        for k in range(2):
+            j = row(steps, turn, k)
+            pl.when(j != bcol)(
+                lambda j=j: send(cf.at[j], xo.at[yl, z], e_s, e_r.at[(j // 8 + yl) % 2], (brow, j))
+            )
 
     for g in range(GROUPS):
         place(g, sm[g], yl)
@@ -350,9 +362,13 @@
             rings[time].step(0)
         if time >= 4 * LAG:
             finish(time - 4 * LAG)
+        for k in range(OUT_LATER):
+            if OUT_TIME[k] == time:
+                out(*GROUPS_DONE[k])
     for turn in range(2):
         cb[(yh + turn) % 2, brow] = cf[row(0, turn, 0)]
-    out()
+    for group in GROUPS_DONE[OUT_LATER:]:
+        out(*group)
     landed(cb.at[:, pl.ds(0, 15)], b_r)
 
     for k in range(2):
@@ -402,7 +418,7 @@
 
     for k in range(2):
         pl.when(from_afar(k))(lambda k=k: landed(fr.at[k], h_r.at[k]))
-        ojj[k] = d_ref[k] - fr[k].T
+        ojj[k] = fr[k].T
 
     for h in range(2):
         pl.when(away(h))(lambda h=h: home(h).wait_send())
@@ -427,21 +443,25 @@
 
 def on_device(inverse_block, panels, ancestor_blocks, pattern, diag_inverse):
     vmem, smem = pl.BlockSpec(memory_space=pltpu.VMEM), pl.BlockSpec(memory_space=pltpu.SMEM)
+    hbm = pl.BlockSpec(memory_space=pl.ANY)
     dma = pltpu.SemaphoreType.DMA
     count = len(UNITS)
     semaphores = [
         (4,), (4,), (GROUPS,), (GROUPS,), (), (2, 4), (), (4,), (), (4, 2), (count,), (count, 2, 4), (), (), (), (2,),
         (), (2, 2, 4), (2,), (2,), (), (2,), (), (), (), (2, 2), (), (2,), (), (4, 1),
     ]
-    return pl.pallas_call(
+    product, diagonal = pl.pallas_call(
         kernel,
         out_shape=(
             jax.ShapeDtypeStruct((2, ROWS, COLS), F32),
             jax.ShapeDtypeStruct((2, COLS, COLS), F32),
         ),
-        in_specs=[vmem, vmem, smem, smem, vmem],
+        in_specs=[hbm, hbm, smem, smem],
         out_specs=(vmem, vmem),
         scratch_shapes=[
+            pltpu.VMEM((ROWS, ROWS), F32),
+            pltpu.VMEM((2, ROWS, COLS), F32),
+            dma((2,)),
             pltpu.VMEM((ROWS, COLS), F32),
             pltpu.VMEM((GROUPS, TALL, ROWS), F32),
             pltpu.VMEM((GROUPS, TALL, ROWS), F32),
@@ -471,7 +491,8 @@
         ),
         cost_estimate=pl.CostEstimate(flops=8 * 10**9, bytes_accessed=3 * 2**20, transcendentals=0),
         name="selected_inverse",
-    )(inverse_block, panels, ancestor_blocks, pattern, diag_inverse)
+    )(inverse_block, panels, ancestor_blocks, pattern)
+    return -product, diag_inverse + diagonal
 
 
 def solution(mesh):

time: 128 us -> 127 us (level)
  the two profiles are of different devices: /device:TPU:5 before, /device:TPU:25 now
where the time goes in v5:
time: 127 us
  Pallas kernels  124 us (98%)
  other arithmetic  2.58 us (2%)
    pallas_call x1, Pallas kernels, on_device(): pl.pallas_call(kernel, out_shape=(jax.ShapeDtypeStruct((2, ROWS, COLS), F...  124 us

profile of v5, /device:TPU:25, one launch (start us, length us, event | category | flops | bytes accessed | tf_op | source)
XLA Modules:
  0.0 127.1 jit_solution(14936981661168743528)
XLA Ops:
  0.6 123.8 %selected_inverse.1 = (f32[2,512,128]{2,1,0:T(8,128)}, f32[2,128,128]{2,1,0:T(8,128)}) custom-call(f32[512,512]{1,0:T(8,128)} %s_hbm.1, f32[2,512,128]{2,1,0:T(8,128)} %p_hbm.1, s32[2,32]{1,0:T(2,128)} %anc.1, s32[2,2]{1,0:T(2,128)} %pat.1), custom_call_target="tpu_custom_call" | custom-call | flops 8000000000 | bytes 3145728 | tf_op jit(solution)/shard_map/selected_inverse/pallas_call | solution.py:453
  124.5 0.0 copy-start
  124.5 0.0 copy-start.1
  124.5 1.9 %neg.3 = f32[2,512,128]{2,1,0:T(8,128)} negate(f32[2,512,128]{2,1,0:T(8,128)} %get-tuple-element.4) | non-fusion elementwise | flops 131072 | bytes 1048576 | tf_op jit(solution)/shard_map/neg | solution.py:495
  126.4 0.0 copy-done
  126.4 0.0 copy-done.1
  126.4 0.7 add.3
Async XLA Ops:
  124.5 1.9 %copy-start = (f32[2,128,128]{2,1,0:T(8,128)S(1)}, f32[2,128,128]{2,1,0:T(8,128)}, u32[]{:S(2)}) copy-start(f32[2,128,128]{2,1,0:T(8,128)} %param.9) | copy-start | bytes 393220
  124.5 1.9 %copy-start.1 = (f32[2,128,128]{2,1,0:T(8,128)S(1)}, f32[2,128,128]{2,1,0:T(8,128)}, u32[]{:S(2)}) copy-start(f32[2,128,128]{2,1,0:T(8,128)} %get-tuple-element.5) | copy-start | bytes 393220
